TPU v7x, 128 devices: a whole 4x4x4 slice. The times are simulated.
128 devices in a mesh: fsdp: 32 (over z, x, core), grp: 4 (over y).
Axes of the slice: x: 4, y: 4, z: 4, core: 2. Of those that a mesh axis runs over, the one named last changes fastest.
Arguments:
- grad: bfloat16 [64, 1024, 1024], P(None, 'fsdp')
- adam_second: float32 [64, 1024, 1024], P(None, 'fsdp', 'grp'), may hold values from 0.002 to 0.05
- left_statistic_matrix: float32 [96, 1024, 1024], P('fsdp', 'grp'), may hold values from -4 to 4
- right_statistic_matrix: float32 [96, 1024, 1024], P('fsdp', 'grp'), may hold values from -4 to 4
- left_root: bfloat16 [96, 1024, 1024], P('fsdp', 'grp'), as said below
- right_root: bfloat16 [96, 1024, 1024], P('fsdp', 'grp'), as said below
- slot_of_block: int32 [64], replicated, may hold values from 0 to 95, as said below
Outputs:
- left_new: float32 [96, 1024, 1024], P('fsdp', 'grp')
- right_new: float32 [96, 1024, 1024], P('fsdp', 'grp')
- second_new: float32 [64, 1024, 1024], P(None, 'fsdp', 'grp')
- direction: float32 [64, 1024, 1024], P(None, 'fsdp', 'grp')
Inputs may be any that keep to these rules, and one draw needn't show every extreme that they name: `slot_of_block`: entries are distinct. Slot s belongs to the owner s // 3 along fsdp; some owner has all 3 of its slots named. `left_root`: each slot's matrix is symmetric. `right_root`: each slot's matrix is symmetric.
All inputs are finite; a program needn't handle non-finite values.
Results may differ from a plain program's by a relative error of at most 0.0029.
Values may be sent and summed in bfloat16 or wider, within the bound.
A program may use at most 128 MiB of HBM per device.

v0:
```python
import jax
import jax.numpy as jnp
from jax import lax
from jax.sharding import PartitionSpec as P


def per_device(
    grad,
    adam_second,
    left_statistic_matrix,
    right_statistic_matrix,
    left_root,
    right_root,
    slot_of_block,
):
    fsdp_count = lax.axis_size("fsdp")
    member = lax.axis_index("grp")
    owner = lax.axis_index("fsdp")
    blocks, rows_here, order = grad.shape
    share = adam_second.shape[2]
    slots_here = left_statistic_matrix.shape[0]
    total_slots = slots_here * fsdp_count
    cells = float(order * order)
    columns = lax.dynamic_slice_in_dim(grad, member * share, share, 2)
    widened = columns.astype(jnp.float32)
    second_new = 0.95 * adam_second + 0.05 * widened * widened
    adam = widened / (jnp.sqrt(second_new) + 1e-08)
    adam_part = jnp.sum(adam * adam, axis=(1, 2))
    packed = jnp.zeros((total_slots, rows_here, order), jnp.bfloat16).at[slot_of_block].set(grad)
    slot_grad = lax.all_to_all(packed, "fsdp", split_axis=0, concat_axis=1, tiled=True)
    own_rows = lax.dynamic_slice_in_dim(slot_grad, member * share, share, 1)
    own_cols = lax.dynamic_slice_in_dim(slot_grad, member * share, share, 2)
    left_new = 0.9 * left_statistic_matrix + 0.1 * jnp.einsum(
        "srk,sck->src", own_rows, slot_grad, preferred_element_type=jnp.float32
    )
    right_new = 0.9 * right_statistic_matrix + 0.1 * jnp.einsum(
        "skr,skc->src", own_cols, slot_grad, preferred_element_type=jnp.float32
    )
    half_columns = jnp.einsum(
        "sik,sck->sic", slot_grad, right_root, preferred_element_type=jnp.float32
    ).astype(jnp.bfloat16)
    shampoo_columns = jnp.einsum(
        "srk,skc->src",
        lax.all_gather(left_root, "grp", axis=1, tiled=True),
        half_columns,
        preferred_element_type=jnp.float32,
    )
    shampoo_part = jnp.sum(shampoo_columns * shampoo_columns, axis=(1, 2))
    my_slots = owner * slots_here + jnp.arange(slots_here, dtype=jnp.int32)
    owned = (slot_of_block[None, :] == my_slots[:, None]).astype(jnp.float32)
    adam_total = lax.psum(adam_part, ("fsdp", "grp"))
    shampoo_total = lax.psum(shampoo_part, "grp")
    adam_slot = jnp.sum(owned * adam_total[None, :], axis=1)
    slot_factor = jnp.sqrt(adam_slot / cells / (shampoo_total / cells + 1e-06))
    outgoing = shampoo_columns * slot_factor[:, None, None]
    returned = lax.all_to_all(outgoing, "fsdp", split_axis=1, concat_axis=0, tiled=True)
    direction = returned[slot_of_block]
    return (left_new, right_new, second_new, direction)


def solution(mesh):
    return jax.shard_map(
        per_device,
        mesh=mesh,
        in_specs=(
            P(None, "fsdp", None),
            P(None, "fsdp", "grp"),
            P("fsdp", "grp", None),
            P("fsdp", "grp", None),
            P("fsdp", "grp", None),
            P("fsdp", "grp", None),
            P(),
        ),
        out_specs=(
            P("fsdp", "grp", None),
            P("fsdp", "grp", None),
            P(None, "fsdp", "grp"),
            P(None, "fsdp", "grp"),
        ),
        check_vma=False,
    )
```

profile of v0, /device:TPU:1, one launch (start us, length us, event | category | flops | bytes accessed | tf_op | source)
XLA Modules:
  0.0 271.8 jit_solution(448499590776414024)
XLA Ops:
  7.2 0.0 copy-start
  7.2 0.0 all-gather.2.cloned.1.call-start
  7.2 0.7 all-gather.2.cloned.1.call-update
  7.9 0.7 compare_select_fusion
  8.6 3.5 %broadcast_in_dim.4 = bf16[96,32,1024]{2,1,0:T(8,128)(2,1)} broadcast(bf16[]{:T(256)} %constant.6.clone.1), dimensions={} | broadcast | bytes 6291458 | tf_op jit(solution)/shard_map/broadcast_in_dim | solution.py:29
  12.0 12.2 %scatter_fusion = bf16[96,32,1024]{2,1,0:T(8,128)(2,1)} fusion(bf16[96,32,1024]{2,1,0:T(8,128)(2,1)} %broadcast_in_dim.4, s32[64]{0:T(128)S(1)} %compare_select_fusion, bf16[64,32,1024]{2,1,0:T(8,128)(2,1)} %param.7), kind=kCustom, calls=%fused_computation.1 | custom fusion | bytes 12583168 | tf_op jit(solution)/shard_map/scatter | solution.py:29
  24.3 9.6 %all-to-all-start = ((bf16[96,32,1024]{2,1,0:T(8,128)(2,1)}), bf16[96,32,1024]{2,1,0:T(8,128)(2,1)}, u32[]{:S(2)}, u32[]{:S(2)}) async-start(bf16[96,32,1024]{2,1,0:T(8,128)(2,1)} %scatter_fusion), calls=%async_computation | async-start | bytes 12582912 | tf_op jit(solution)/shard_map/all_to_all | solution.py:30
  33.9 0.0 copy-start.3
  33.9 4.5 %fusion.2 = (f32[64]{0:T(128)S(1)}, f32[64,32,256]{2,1,0:T(8,128)}) fusion(bf16[64,32,1024]{2,1,0:T(8,128)(2,1)} %param.7, s32[]{:T(128)S(6)} %select_n.10, f32[64,32,256]{2,1,0:T(8,128)} %param.8), kind=kLoop, calls=%fused_computation.10 | loop fusion | flops 4718528 | bytes 5243140 | tf_op jit(solution)/shard_map/reduce_sum | solution.py:28
  38.4 126.4 %psum.14 = f32[64]{0:T(128)S(1)} all-reduce(f32[64]{0:T(128)S(1)} %get-tuple-element.4), channel_id=1, replica_groups=mesh['fsdp'=32,'grp'=4] {'fsdp','grp'}, use_global_device_ids=true, to_apply=%region_2.0 | all-reduce | flops 64 | bytes 512 | tf_op jit(solution)/shard_map/psum | solution.py:51
  164.8 0.0 copy-done.3
  164.8 0.2 select_reduce_fusion
  165.0 0.0 all-to-all-done
  165.0 6.8 %copy.22 = bf16[3,32,32,1024]{3,2,1,0:T(8,128)(2,1)} copy(bf16[3,32,32,1024]{3,2,0,1:T(8,128)(2,1)} %bitcast.1) | data formatting | bytes 12582912 | tf_op jit(solution)/shard_map/all_to_all | solution.py:30
  171.8 0.0 all-gather.2.cloned.1.call-done
  171.8 0.0 copy-done
  171.8 9.8 %multiply_reduce_fusion = (f32[3]{0:T(128)S(1)}, f32[3,256,1024]{2,1,0:T(8,128)}) fusion(bf16[3,1024,1024]{2,1,0:T(8,128)(2,1)} %all-gather.2.cloned.1.call-done, bf16[3,1024,1024]{2,1,0:T(8,128)(2,1)} %bitcast.15, bf16[3,256,1024]{2,1,0:T(8,128)(2,1)S(1)} %copy-done), kind=kOutput, calls=%fused_computation.3 | convolution fusion | flops 3223584768 | bytes 17301516 | tf_op jit(solution)/shard_map/srk,skc->src/dot_general | solution.py:42
  181.5 7.9 %psum.15 = f32[3]{0:T(128)S(1)} all-reduce(f32[3]{0:T(128)S(1)} %get-tuple-element.6), channel_id=1, replica_groups=mesh['fsdp'=32,'grp'=4] {'grp'}, use_global_device_ids=true, to_apply=%region_5.0 | all-reduce | flops 3 | bytes 24 | tf_op jit(solution)/shard_map/psum | solution.py:52
  189.5 4.2 %multiply_bitcast_fusion = f32[3,1024,256]{1,2,0:T(8,128)} fusion(f32[3,256,1024]{2,1,0:T(8,128)} %get-tuple-element.7, f32[3]{0:T(128)S(1)} %fusion.8), kind=kLoop, calls=%fused_computation.2 | loop fusion | flops 786432 | bytes 6291468 | tf_op jit(solution)/shard_map/mul | solution.py:55
  193.6 5.0 %copy.25 = f32[3,1024,256]{2,0,1:T(4,128)} copy(f32[3,1024,256]{1,2,0:T(8,128)} %multiply_bitcast_fusion) | data formatting | bytes 6291456 | tf_op jit(solution)/shard_map/mul | solution.py:55
  198.7 7.4 %all-to-all-start.1 = ((f32[3,1024,256]{2,0,1:T(4,128)}), f32[3,1024,256]{2,0,1:T(4,128)}, u32[]{:S(2)}, u32[]{:S(2)}) async-start(f32[3,1024,256]{2,0,1:T(4,128)} %copy.25), calls=%async_computation.1 | async-start | bytes 8388608 | tf_op jit(solution)/shard_map/all_to_all | solution.py:56
  206.2 0.0 copy-start.2
  206.2 8.1 %multiply_add_fusion = f32[3,256,1024]{2,1,0:T(8,128)} fusion(f32[3,256,1024]{2,1,0:T(8,128)} %param.10, bf16[3,1024,1024]{2,1,0:T(8,128)(2,1)} %bitcast.16, s32[]{:T(128)S(6)} %select_n.10), kind=kOutput, calls=%fused_computation.5 | convolution fusion | flops 1612972032 | bytes 14155780 | tf_op jit(solution)/shard_map/skr,skc->src/dot_general | solution.py:36
  214.3 0.0 copy-done.2
  214.3 7.0 %multiply_add_fusion.1 = f32[3,256,1024]{2,1,0:T(8,128)} fusion(f32[3,256,1024]{2,1,0:T(8,128)S(1)} %copy-done.2, bf16[3,1024,1024]{2,1,0:T(8,128)(2,1)} %bitcast.17, s32[]{:T(128)S(6)} %select_n.10), kind=kOutput, calls=%fused_computation.6 | convolution fusion | flops 1612972032 | bytes 14155780 | tf_op jit(solution)/shard_map/srk,sck->src/dot_general | solution.py:33
  221.3 35.1 %all-to-all-done.1 = f32[3,1024,256]{2,0,1:T(4,128)} async-done(((f32[3,1024,256]{2,0,1:T(4,128)}), f32[3,1024,256]{2,0,1:T(4,128)}, u32[]{:S(2)}, u32[]{:S(2)}) %all-to-all-start.1) | async-done | bytes 3145760 | tf_op jit(solution)/shard_map/all_to_all | solution.py:56
  256.4 2.8 %copy.26 = f32[3,1024,256]{2,1,0:T(8,128)S(1)} copy(f32[3,1024,256]{2,0,1:T(4,128)} %all-to-all-done.1) | data formatting | bytes 6291456 | tf_op jit(solution)/shard_map/all_to_all | solution.py:56
  259.2 0.0 copy-start.1
  259.2 1.9 copy.27
  261.1 3.9 %gather_fusion = f32[64,32,256]{2,1,0:T(8,128)} fusion(f32[96,32,256]{2,1,0:T(8,128)} %bitcast.19, s32[1024]{0:T(1024)S(1)} %pad_clamp_fusion), kind=kCustom, calls=%fused_computation | custom fusion | bytes 4194560 | tf_op jit(solution)/shard_map/gather | solution.py:57
  265.0 0.0 copy-done.1
  (3 shorter events, 0.0 us)
Async XLA Ops:
  7.2 164.6 %copy-start = (bf16[3,256,1024]{2,1,0:T(8,128)(2,1)S(1)}, bf16[3,256,1024]{2,1,0:T(8,128)(2,1)}, u32[]{:S(2)}) copy-start(bf16[3,256,1024]{2,1,0:T(8,128)(2,1)} %param.12) | copy-start | bytes 4718596
  7.2 164.6 %all-gather.2.cloned.1.call-start = ((), (), s32[]{:S(2)}) async-start(), calls=%async_computation.2 | async-start | bytes 7864320 | tf_op jit(solution)/shard_map/all_gather | solution.py:44
  24.3 140.7 %all-to-all-start = ((bf16[96,32,1024]{2,1,0:T(8,128)(2,1)}), bf16[96,32,1024]{2,1,0:T(8,128)(2,1)}, u32[]{:S(2)}, u32[]{:S(2)}) async-start(bf16[96,32,1024]{2,1,0:T(8,128)(2,1)} %scatter_fusion), calls=%async_computation | async-start | bytes 12582912 | tf_op jit(solution)/shard_map/all_to_all | solution.py:30
  33.9 130.9 %copy-start.3 = (s32[64]{0:T(128)S(1)}, s32[64]{0:T(128)}, u32[]{:S(2)}) copy-start(s32[64]{0:T(128)} %param.13) | copy-start | bytes 772
  198.7 57.7 %all-to-all-start.1 = ((f32[3,1024,256]{2,0,1:T(4,128)}), f32[3,1024,256]{2,0,1:T(4,128)}, u32[]{:S(2)}, u32[]{:S(2)}) async-start(f32[3,1024,256]{2,0,1:T(4,128)} %copy.25), calls=%async_computation.1 | async-start | bytes 8388608 | tf_op jit(solution)/shard_map/all_to_all | solution.py:56
  206.2 8.1 %copy-start.2 = (f32[3,256,1024]{2,1,0:T(8,128)S(1)}, f32[3,256,1024]{2,1,0:T(8,128)}, u32[]{:S(2)}) copy-start(f32[3,256,1024]{2,1,0:T(8,128)} %param.9) | copy-start | bytes 9437188
  259.2 5.8 %copy-start.1 = (bf16[3,256,1024]{2,1,0:T(8,128)(2,1)S(1)}, bf16[3,256,1024]{2,1,0:T(8,128)(2,1)}, u32[]{:S(2)}) copy-start(bf16[3,256,1024]{2,1,0:T(8,128)(2,1)} %param.12) | copy-start | bytes 4718596
Sparse Core Ops, SparseCore 0:
  9.7 69.0 all-gather.1
where the time goes:
time: 275 us; the launch traced here: 272 us
  blocking collectives  134 us (49%)
  local copies, waits for them, and re-layouts  36.1 us (13%)
  waiting for transfers between devices  35.8 us (13%)
  matrix products  24.9 us (9%)
  starting transfers between devices  17.1 us (6%)
  between operations  14.1 us (5%)
  other arithmetic  9.51 us (3%)
    psum x1, blocking collectives, per_device(): adam_total = lax.psum(adam_part, ('fsdp', 'grp'))  126 us
    all_to_all x1, waiting for transfers between devices, per_device(): lax.all_to_all(outgoing, 'fsdp', split_axis=1, concat_axis=0, tiled=True)  35.1 us
    scatter x1, local copies, waits for them, and re-layouts, per_device(): jnp.zeros((total_slots, rows_here, order), jnp.bfloat16).at[slot_of_block]  12.2 us
    dot_general x1, matrix products, per_device(): jnp.einsum('srk,skc->src', lax.all_gather(left_root, 'grp', axis=1, tiled...  9.77 us
    all_to_all x1, starting transfers between devices, per_device(): lax.all_to_all(packed, 'fsdp', split_axis=0, concat_axis=1, tiled=True)  9.61 us
    dot_general x1, matrix products, per_device(): jnp.einsum('skr,skc->src', own_cols, slot_grad, preferred_element_type=jn...  8.11 us
    psum x1, blocking collectives, per_device(): shampoo_total = lax.psum(shampoo_part, 'grp')  7.93 us
    all_to_all x1, starting transfers between devices, per_device(): lax.all_to_all(outgoing, 'fsdp', split_axis=1, concat_axis=0, tiled=True)  7.45 us
  transfers between devices with their start and end apart: 3, of which 1 were waited for; matrix products, arithmetic and copies ran while one was open for 16% of the time, Pallas kernels for 0%

commit v1 on v0

v1 whole, which is shorter than its diff:
```python
import functools

import jax
import jax.numpy as jnp
from jax import lax
from jax.experimental import pallas as pl
from jax.experimental.pallas import tpu as pltpu
from jax.sharding import PartitionSpec as P

MESH = pl.DeviceIdType.MESH
F32, BF16 = jnp.float32, jnp.bfloat16
NT = (((1,), (1,)), ((), ()))
TN = (((0,), (0,)), ((), ()))
VMEM_LIMIT = 60 * 2**20


def exchange_kernel(
    table, grad, second, left, right, left_root, right_root,
    left_out, right_out, second_out, returned_out, sums_out,
    blocks, cols, sec, lstat, rstat, packed, whole, roots, rown, rnext, half,
    sent, handed, got, stat_out, stat_in, adam, sham, tile, tiles_in,
    sem_in, sem_g, sem_gs, sem_l, sem_ls, sem_r, sem_rs, sem_s, sem_ss, sem_h, sem_hs, sem_p, sem_ps,
    sem_t, sem_ts, sem_out,
):
    f, y = lax.axis_index("fsdp"), lax.axis_index("grp")
    c, x, z = f % 2, (f // 2) % 4, f // 8
    step = 1 - 2 * c
    up, down, across = (y + step + 4) % 4, (y - step + 4) % 4, (y + 2) % 4
    order = 1024
    share = 256
    rows = 32

    def device(zz, xx, cc):
        return zz * 8 + xx * 2 + cc

    def does(j):
        return (y + c + j) % 2 == 0

    def remote(src, dst, send, recv, ff, yy):
        return pltpu.make_async_remote_copy(
            src_ref=src, dst_ref=dst, send_sem=send, recv_sem=recv, device_id=(ff, yy), device_id_type=MESH
        )

    def wait_bytes(ref, sem):
        pltpu.make_async_copy(ref, ref, sem).wait()

    mine = pl.ds(pl.multiple_of(y * share, share), share)
    load_blocks = pltpu.make_async_copy(grad, blocks.at[pl.ds(0, 64)], sem_in.at[0])
    load_blocks.start()
    load_cols = pltpu.make_async_copy(grad.at[:, :, mine], cols, sem_in.at[1])
    load_cols.start()
    load_sec = pltpu.make_async_copy(second, sec, sem_in.at[2])
    load_sec.start()
    load_rown = pltpu.make_async_copy(right_root, rown, sem_in.at[3])
    load_rown.start()
    load_left = pltpu.make_async_copy(left, lstat, sem_in.at[4])
    load_left.start()
    load_right = pltpu.make_async_copy(right, rstat, sem_in.at[5])
    load_right.start()

    barrier = pltpu.get_barrier_semaphore()

    def greet(k, carry):
        other = (f + k) % 32
        pl.semaphore_signal(barrier, inc=1, device_id=(other, y), device_id_type=MESH)
        return carry

    lax.fori_loop(1, 32, greet, 0)
    for d in (1, 2, 3):
        pl.semaphore_signal(barrier, inc=1, device_id=(f, (y + d) % 4), device_id_type=MESH)
    blocks[64] = jnp.zeros((rows, order), BF16)
    pl.semaphore_wait(barrier, 34)

    def block_of(j, k):
        return left_root.at[j, :, pl.ds(pl.multiple_of(k * share, share), share)]

    for j in range(3):

        @pl.when(does(j))
        def _():
            remote(block_of(j, y), roots.at[j, y, y], sem_ls.at[j], sem_l.at[j], f, across).start()
            for k in range(4):
                pltpu.make_async_copy(block_of(j, k), roots.at[j, y, k], sem_l.at[j]).start()

        @pl.when(jnp.logical_not(does(j)))
        def _():
            remote(right_root.at[j], rnext.at[j], sem_rs.at[j], sem_r.at[j], f, down).start()
            for k in (y, up, across):
                remote(block_of(j, k), roots.at[j, y, k], sem_ls.at[j], sem_l.at[j], f, down).start()
            for k in (y, down):
                remote(block_of(j, k), roots.at[j, y, k], sem_ls.at[j], sem_l.at[j], f, up).start()

    load_blocks.wait()

    def send_grad(n, carry):
        j, k = n // 16, n % 16
        dz = k % 4
        dx = (k // 4 - dz + 4) % 4
        zz, xx, cc = (z + dz) % 4, (x + dx) % 4, (y + j) % 2
        ff = device(zz, xx, cc)
        packed[n] = blocks[table[ff * 3 + j]]
        target = whole.at[j, pl.ds(pl.multiple_of(f * rows, rows), rows)]

        @pl.when(ff == f)
        def _():
            pltpu.make_async_copy(packed.at[n], target, sem_g.at[j]).start()

        @pl.when(ff != f)
        def _():
            remote(packed.at[n], target, sem_gs.at[j], sem_g.at[j], ff, y).start()

        return carry

    lax.fori_loop(0, 48, send_grad, 0)

    load_cols.wait()
    load_sec.wait()
    adam[...] = jnp.zeros_like(adam)
    sham[...] = jnp.zeros_like(sham)

    def adam_block(b, carry):
        wide = cols[b].astype(F32)
        new = 0.95 * sec[b] + 0.05 * wide * wide
        sec[b] = new
        value = wide / (jnp.sqrt(new) + 1e-08)
        part = jnp.sum(value * value, axis=0, keepdims=True)
        adam[pl.ds(b, 1), :] = part[:, :128] + part[:, 128:]
        return carry

    lax.fori_loop(0, 64, adam_block, 0)
    store_sec = pltpu.make_async_copy(sec, second_out, sem_out.at[0])
    store_sec.start()
    load_rown.wait()

    def fill(j, carry):
        @pl.when(does(j))
        def _():
            wait_bytes(packed.at[pl.ds(0, 20)], sem_l.at[j])
            for r, k in ((up, y), (across, y), (down, y), (across, up), (down, up), (across, down)):
                roots[j, r, k] = roots[j, k, r].T

        return carry

    lax.fori_loop(0, 3, fill, 0)

    def spread(src, j):
        def one(k, carry):
            dz = k % 4
            dx = ((k // 4) % 4 - dz + 4) % 4
            ff = device((z + dz) % 4, (x + dx) % 4, (c + k // 16) % 2)
            piece = src.at[pl.ds(pl.multiple_of(ff * rows, rows), rows)]
            target = got.at[f * 3 + j]

            @pl.when(k == 0)
            def _():
                pltpu.make_async_copy(piece, target, sem_s).start()

            @pl.when(k != 0)
            def _():
                remote(piece, target, sem_ss.at[j], sem_s, ff, y).start()

            return carry

        lax.fori_loop(0, 32, one, 0)

    def columns(j, root, out):
        def product(r, carry):
            at = pl.ds(pl.multiple_of(r * share, share), share)
            half[r] = lax.dot_general(whole[j, at], root[j], NT, preferred_element_type=F32).astype(BF16)
            return carry

        lax.fori_loop(0, 4, product, 0)

        def outer(r, total):
            value = jnp.dot(roots[j, r, 0], half[0], preferred_element_type=F32)
            for k in range(1, 4):
                value += jnp.dot(roots[j, r, k], half[k], preferred_element_type=F32)
            out[pl.ds(pl.multiple_of(r * share, share), share), :] = value.astype(BF16)
            part = jnp.sum(value * value, axis=0, keepdims=True)
            return total + part[:, :128] + part[:, 128:]

        return lax.fori_loop(0, 4, outer, jnp.zeros((1, 128), F32))

    def direct(j, carry):
        @pl.when(does(j))
        def _():
            wait_bytes(rnext.at[j], sem_r.at[j])
            wait_bytes(whole.at[j], sem_g.at[j])
            first = columns(j, rnext, sent.at[j, 1])
            remote(sent.at[j, 1], handed.at[j], sem_hs.at[j], sem_h.at[j], f, up).start()
            other = columns(j, rown, sent.at[j, 0])
            sham[pl.ds(f * 3 + j, 1), :] = first + other
            spread(sent.at[j, 0], j)

        @pl.when(jnp.logical_not(does(j)))
        def _():
            wait_bytes(handed.at[j], sem_h.at[j])
            spread(handed.at[j], j)

        return carry

    lax.fori_loop(0, 3, direct, 0)

    tile[0] = jnp.zeros((8, 128), F32)
    tile[0, 0:1, :] = jnp.sum(adam[...].T, axis=0, keepdims=True)
    tile[0, 1:2, :] = jnp.sum(sham[...].T, axis=0, keepdims=True)
    x_peers = [(device(z, (x + d) % 4, c), y) for d in (1, 2, 3)]
    z_peers = [(device((z + d) % 4, x, c), y) for d in (1, 2, 3)]
    c_peers = [(device(z, x, 1 - c), y)]
    y_peers = [(f, (y + d) % 4) for d in (1, 2, 3)]
    stages = [x_peers, z_peers, c_peers, y_peers]

    def stage_copies(s):
        return [
            remote(tile.at[s], tiles_in.at[s, n], sem_ts.at[s, n], sem_t.at[s, n], *peer)
            for n, peer in enumerate(stages[s])
        ]

    def start_stage(s):
        for copy in stage_copies(s):
            copy.start()

    def end_stage(s):
        for copy in stage_copies(s):
            copy.wait()
        total = tile[s]
        for n in range(len(stages[s])):
            total += tiles_in[s, n]
        tile[s + 1] = total

    start_stage(0)

    load_left.wait()
    load_right.wait()

    def statistics(j, carry):
        @pl.when(does(j))
        def _():
            def rows_of(r):
                at = pl.ds(pl.multiple_of(r * share, share), share)
                lhs = whole[j, at]
                return lax.dot_general(lhs, whole[j], NT, preferred_element_type=F32)

            def cols_of(r):
                at = pl.ds(pl.multiple_of(r * share, share), share)
                lhs = whole[j, :, at].T
                return jnp.dot(lhs, whole[j], preferred_element_type=F32)

            stat_out[j, 0] = rows_of(up).astype(BF16)
            stat_out[j, 1] = cols_of(up).astype(BF16)
            remote(stat_out.at[j], stat_in.at[j], sem_ps.at[j], sem_p.at[j], f, up).start()
            lstat[j] = 0.9 * lstat[j] + 0.1 * rows_of(y)
            rstat[j] = 0.9 * rstat[j] + 0.1 * cols_of(y)

        return carry

    lax.fori_loop(0, 3, statistics, 0)
    end_stage(0)
    start_stage(1)

    def receive(j, carry):
        @pl.when(jnp.logical_not(does(j)))
        def _():
            wait_bytes(stat_in.at[j], sem_p.at[j])
            lstat[j] = 0.9 * lstat[j] + 0.1 * stat_in[j, 0].astype(F32)
            rstat[j] = 0.9 * rstat[j] + 0.1 * stat_in[j, 1].astype(F32)

        return carry

    lax.fori_loop(0, 3, receive, 0)
    store_left = pltpu.make_async_copy(lstat, left_out, sem_out.at[1])
    store_left.start()
    store_right = pltpu.make_async_copy(rstat, right_out, sem_out.at[2])
    store_right.start()
    end_stage(1)
    start_stage(2)
    end_stage(2)
    start_stage(3)
    end_stage(3)
    store_sums = pltpu.make_async_copy(tile.at[4], sums_out, sem_out.at[3])
    store_sums.start()

    for j in range(3):

        @pl.when(does(j))
        def _():
            wait_bytes(packed.at[pl.ds(0, 15)], sem_gs.at[j])
            wait_bytes(roots.at[j, 0, 0], sem_ls.at[j])
            wait_bytes(sent.at[j, 1], sem_hs.at[j])
            wait_bytes(stat_out.at[j], sem_ps.at[j])

        @pl.when(jnp.logical_not(does(j)))
        def _():
            wait_bytes(packed.at[pl.ds(0, 16)], sem_gs.at[j])
            wait_bytes(rnext.at[j], sem_rs.at[j])
            wait_bytes(packed.at[pl.ds(0, 10)], sem_ls.at[j])

        wait_bytes(got.at[pl.ds(0, 31)], sem_ss.at[j])
    wait_bytes(got, sem_s)
    store_got = pltpu.make_async_copy(got, returned_out, sem_out.at[4])
    store_got.start()
    store_got.wait()
    store_sec.wait()
    store_left.wait()
    store_right.wait()
    store_sums.wait()


def direction_kernel(slots, sums, returned, out):
    step = pl.program_id(0)
    for n in range(8):
        b = step * 8 + n
        slot = slots[b]
        adam_sq = jnp.full((1, 128), sums[0, b], F32) * (1.0 / 1048576.0)
        sham_sq = jnp.full((1, 128), sums[1, slot], F32) * (1.0 / 1048576.0)
        factor = jnp.sqrt(adam_sq / (sham_sq + 1e-06))
        wide = returned[slot].astype(F32)
        out[n, :, :128] = wide[:, :128] * factor
        out[n, :, 128:] = wide[:, 128:] * factor


def per_device(grad, second, left, right, left_root, right_root, slot_of_block):
    any_space = pl.BlockSpec(memory_space=pl.ANY)
    slots = jnp.arange(96, dtype=jnp.int32)
    named = slot_of_block[None, :] == slots[:, None]
    table = jnp.min(jnp.where(named, jnp.arange(64, dtype=jnp.int32)[None, :], 64), axis=1)
    dma = pltpu.SemaphoreType.DMA
    left_new, right_new, second_new, returned, sums = pl.pallas_call(
        exchange_kernel,
        name="exchange",
        out_shape=(
            jax.ShapeDtypeStruct((3, 256, 1024), F32),
            jax.ShapeDtypeStruct((3, 256, 1024), F32),
            jax.ShapeDtypeStruct((64, 32, 256), F32),
            jax.ShapeDtypeStruct((96, 32, 256), BF16),
            jax.ShapeDtypeStruct((8, 128), F32),
        ),
        in_specs=[pl.BlockSpec(memory_space=pltpu.SMEM)] + [any_space] * 6,
        out_specs=(any_space,) * 5,
        scratch_shapes=[
            pltpu.VMEM((65, 32, 1024), BF16),
            pltpu.VMEM((64, 32, 256), BF16),
            pltpu.VMEM((64, 32, 256), F32),
            pltpu.VMEM((3, 256, 1024), F32),
            pltpu.VMEM((3, 256, 1024), F32),
            pltpu.VMEM((48, 32, 1024), BF16),
            pltpu.VMEM((3, 1024, 1024), BF16),
            pltpu.VMEM((3, 4, 4, 256, 256), BF16),
            pltpu.VMEM((3, 256, 1024), BF16),
            pltpu.VMEM((3, 256, 1024), BF16),
            pltpu.VMEM((4, 256, 256), BF16),
            pltpu.VMEM((3, 2, 1024, 256), BF16),
            pltpu.VMEM((3, 1024, 256), BF16),
            pltpu.VMEM((96, 32, 256), BF16),
            pltpu.VMEM((3, 2, 256, 1024), BF16),
            pltpu.VMEM((3, 2, 256, 1024), BF16),
            pltpu.VMEM((128, 128), F32),
            pltpu.VMEM((128, 128), F32),
            pltpu.VMEM((5, 8, 128), F32),
            pltpu.VMEM((4, 3, 8, 128), F32),
            dma((6,)),
            dma((3,)), dma((3,)),
            dma((3,)), dma((3,)),
            dma((3,)), dma((3,)),
            dma, dma((3,)),
            dma((3,)), dma((3,)),
            dma((3,)), dma((3,)),
            dma((4, 3)), dma((4, 3)),
            dma((5,)),
        ],
        compiler_params=pltpu.CompilerParams(
            collective_id=0, has_side_effects=True, vmem_limit_bytes=VMEM_LIMIT
        ),
    )(table, grad, second, left, right, left_root, right_root)
    direction = pl.pallas_call(
        direction_kernel,
        name="direction",
        grid=(8,),
        out_shape=jax.ShapeDtypeStruct((64, 32, 256), F32),
        in_specs=[
            pl.BlockSpec(memory_space=pltpu.SMEM),
            pl.BlockSpec(memory_space=pltpu.SMEM),
            pl.BlockSpec((96, 32, 256), lambda i: (0, 0, 0)),
        ],
        out_specs=pl.BlockSpec((8, 32, 256), lambda i: (i, 0, 0)),
    )(slot_of_block, sums, returned)
    return (left_new, right_new, second_new, direction)


def solution(mesh):
    return jax.shard_map(
        per_device,
        mesh=mesh,
        in_specs=(
            P(None, "fsdp", None),
            P(None, "fsdp", "grp"),
            P("fsdp", "grp", None),
            P("fsdp", "grp", None),
            P("fsdp", "grp", None),
            P("fsdp", "grp", None),
            P(),
        ),
        out_specs=(
            P("fsdp", "grp", None),
            P("fsdp", "grp", None),
            P(None, "fsdp", "grp"),
            P(None, "fsdp", "grp"),
        ),
        check_vma=False,
    )
```

time: 275 us -> 115 us (0.42); the launches traced: 272 us -> 115 us
  blocking collectives: 134 us -> 0 us
  Pallas kernels: 0 us -> 106 us
  waiting for transfers between devices: 35.8 us -> 0 us
  local copies, waits for them, and re-layouts: 36.1 us -> 7.07 us
  matrix products: 24.9 us -> 0 us
  starting transfers between devices: 17.1 us -> 0 us
  between operations: 14.1 us -> 0.65 us
  other arithmetic: 9.51 us -> 1.26 us
    psum x2 -> x0, blocking collectives: 134 us -> none  [the longest x1 126 us: per_device(): adam_total = lax.psum(adam_part, ('fsdp', 'grp'))]
    pallas_call x0 -> x2, Pallas kernels: none -> 106 us  [the longest x1 101 us: per_device(): pl.pallas_call(exchange_kernel, name='exchange', out_shape=(jax.ShapeDtyp...]
    all_to_all x2 -> x0, waiting for transfers between devices: 35.1 us -> none  [the longest x1 35.1 us: per_device(): lax.all_to_all(outgoing, 'fsdp', split_axis=1, concat_axis=0, tiled=True)]
    dot_general x3 -> x0, matrix products: 24.9 us -> none  [the longest x1 9.77 us: per_device(): jnp.einsum('srk,skc->src', lax.all_gather(left_root, 'grp', axis=1, tiled...]
    all_to_all x2 -> x0, starting transfers between devices: 17.1 us -> none  [the longest x1 9.61 us: per_device(): lax.all_to_all(packed, 'fsdp', split_axis=0, concat_axis=1, tiled=True)]
    scatter x1 -> x0, local copies, waits for them, and re-layouts: 12.2 us -> none  [per_device(): jnp.zeros((total_slots, rows_here, order), jnp.bfloat16).at[slot_of_block]]
    all_to_all x3 -> x0, local copies, waits for them, and re-layouts: 11.5 us -> none  [the longest x1 6.77 us: per_device(): lax.all_to_all(packed, 'fsdp', split_axis=0, concat_axis=1, tiled=True)]
    unnamed x8 -> x9, local copies, waits for them, and re-layouts: 0.03 us -> 7.07 us
  transfers between devices with their start and end apart: 3 -> 0, of which waited for: 1 -> 0; matrix products, arithmetic and copies ran while one was open for 16% -> 0% of each run, Pallas kernels for 0% -> 0%
where the time goes in v1:
time: 115 us
  Pallas kernels  106 us (92%)
  local copies, waits for them, and re-layouts  7.07 us (6%)
  other arithmetic  1.26 us (1%)
    pallas_call x1, Pallas kernels, per_device(): pl.pallas_call(exchange_kernel, name='exchange', out_shape=(jax.ShapeDtyp...  101 us
    unnamed x9, local copies, waits for them, and re-layouts  7.07 us
    pallas_call x1, Pallas kernels, per_device(): pl.pallas_call(direction_kernel, name='direction', grid=(8,), out_shape=j...  4.72 us

profile of v1, /device:TPU:1, one launch (start us, length us, event | category | flops | bytes accessed | tf_op | source)
XLA Modules:
  0.0 115.2 jit_solution(15296019079522112400)
XLA Ops:
  0.6 1.3 %select_reduce_fusion.table = s32[96]{0:T(128)} fusion(s32[64]{0:T(128)} %slots.1), kind=kLoop, calls=%fused_computation | loop fusion | flops 18336 | bytes 640 | tf_op jit(solution)/shard_map/reduce_min | solution.py:326
  1.9 101.5 %exchange.1 = (f32[3,256,1024]{2,1,0:T(8,128)}, f32[3,256,1024]{2,1,0:T(8,128)}, f32[64,32,256]{2,1,0:T(8,128)}, bf16[96,32,256]{2,1,0:T(8,128)(2,1)}, f32[8,128]{1,0:T(8,128)}) custom-call(s32[96]{0:T(128)} %select_reduce_fusion.table, bf16[64,32,1024]{2,1,0:T(8,128)(2,1)} %grad.1, f32[64,32,256]{2,1,0:T(8,128)} %second.1, f32[3,256,1024]{2,1,0:T(8,128)} %left.1, ...), custom_call_target="tpu_custom_call" | custom-call | tf_op jit(solution)/shard_map/exchange/pallas_call | solution.py:328
  103.4 0.0 copy-start.1
  103.4 4.7 %direction.1 = f32[64,32,256]{2,1,0:T(8,128)} custom-call(s32[64]{0:T(128)} %slots.1, f32[8,128]{1,0:T(8,128)} %get-tuple-element.12.sums, bf16[96,32,256]{2,1,0:T(8,128)(2,1)} %get-tuple-element.13.returned), custom_call_target="tpu_custom_call" | custom-call | tf_op jit(solution)/shard_map/direction/pallas_call | solution.py:375
  108.1 0.0 copy-done.1
  108.1 0.0 copy-start
  108.1 1.7 %copy.14 = f32[3,256,1024]{2,1,0:T(8,128)} copy(f32[3,256,1024]{2,1,0:T(8,128)S(1)} %copy-done.1) | data formatting | bytes 6291456
  109.8 1.4 %copy-done = f32[3,256,1024]{2,1,0:T(8,128)S(1)} copy-done((f32[3,256,1024]{2,1,0:T(8,128)S(1)}, f32[3,256,1024]{2,1,0:T(8,128)}, u32[]{:S(2)}) %copy-start) | copy-done | bytes 3145752
  111.1 0.0 copy-start.2
  111.1 1.7 %copy.15 = f32[3,256,1024]{2,1,0:T(8,128)} copy(f32[3,256,1024]{2,1,0:T(8,128)S(1)} %copy-done) | data formatting | bytes 6291456
  112.8 1.1 copy-done.2
  113.8 1.3 %copy.16 = f32[64,32,256]{2,1,0:T(8,128)} copy(f32[64,32,256]{2,1,0:T(8,128)S(1)} %copy-done.2) | data formatting | bytes 4194304
Async XLA Ops:
  103.4 4.7 %copy-start.1 = (f32[3,256,1024]{2,1,0:T(8,128)S(1)}, f32[3,256,1024]{2,1,0:T(8,128)}, u32[]{:S(2)}) copy-start(f32[3,256,1024]{2,1,0:T(8,128)} %get-tuple-element.18) | copy-start | bytes 9437188
  108.1 3.0 %copy-start = (f32[3,256,1024]{2,1,0:T(8,128)S(1)}, f32[3,256,1024]{2,1,0:T(8,128)}, u32[]{:S(2)}) copy-start(f32[3,256,1024]{2,1,0:T(8,128)} %get-tuple-element.19) | copy-start | bytes 9437188
  111.1 2.7 %copy-start.2 = (f32[64,32,256]{2,1,0:T(8,128)S(1)}, f32[64,32,256]{2,1,0:T(8,128)}, u32[]{:S(2)}) copy-start(f32[64,32,256]{2,1,0:T(8,128)} %get-tuple-element.20) | copy-start | bytes 6291460

commit v2 on v0

v2 whole, which is shorter than its diff:
```python
import jax
import jax.numpy as jnp
from jax import lax
from jax.experimental import pallas as pl
from jax.experimental.pallas import tpu as pltpu
from jax.sharding import PartitionSpec as P

MESH = pl.DeviceIdType.MESH
F32, BF16 = jnp.float32, jnp.bfloat16
NT = (((1,), (1,)), ((), ()))
EXCHANGE_VMEM = 50 * 2**20
FINISH_VMEM = 16 * 2**20
SHARE, ROWS, ORDER = 256, 32, 1024


def exchange_kernel(
    table, grad, second, left, right, left_root, right_root,
    lstat, rstat, sec, got, sums_out,
    blocks, cols, packed, passing, whole, roots, rown, rnext, half,
    mine, give, relayed, stat_out, stat_in, adam, sham, tile, tiles_in,
    sem_in, sem_g1, sem_g1s, sem_g, sem_gs, sem_l, sem_ls, sem_r, sem_rs,
    sem_h, sem_hs, sem_s1, sem_s1s, sem_s, sem_ss, sem_p, sem_ps, sem_q, sem_qs, sem_t, sem_ts,
):
    f, y = lax.axis_index("fsdp"), lax.axis_index("grp")
    c, x, z = f % 2, (f // 2) % 4, f // 8
    across = (y + 2) % 4

    def device(zz, xx, cc):
        return zz * 8 + xx * 2 + cc

    def does(j):
        return (y + c + j) % 2 == 0

    def up(j):
        return (y + 1 if j == 0 else y + 1 + 2 * c) % 4

    def down(j):
        return (y + 3 if j == 0 else y + 3 + 2 * c) % 4

    def remote(src, dst, send, recv, ff, yy):
        return pltpu.make_async_remote_copy(
            src_ref=src, dst_ref=dst, send_sem=send, recv_sem=recv, device_id=(ff, yy), device_id_type=MESH
        )

    def move(src, dst, send, recv, ff):
        @pl.when(ff == f)
        def _():
            pltpu.make_async_copy(src, dst, recv).start()

        @pl.when(ff != f)
        def _():
            remote(src, dst, send, recv, ff, y).start()

    def wait_units(n, sem):
        ref = blocks.at[pl.ds(0, n)]
        pltpu.make_async_copy(ref, ref, sem).wait()

    def load(src, dst, n):
        copy = pltpu.make_async_copy(src, dst, sem_in.at[n])
        copy.start()
        return copy

    load_blocks = load(grad, blocks.at[pl.ds(0, 64)], 0)
    for j in range(3):
        for k in range(4):
            load(left_root.at[j, :, pl.ds(k * SHARE, SHARE)], roots.at[j * 16 + y * 4 + k], 1)
    load_rown = load(right_root, rown, 2)
    load_cols = load(grad.at[:, :, pl.ds(pl.multiple_of(y * SHARE, SHARE), SHARE)], cols, 3)
    load_sec = load(second, sec, 4)
    load_left = load(left, lstat, 5)
    load_right = load(right, rstat, 6)

    x_line = [(device(z, (x + d) % 4, c), y) for d in (1, 2, 3)]
    x_line += [(device(z, (x + d) % 4, 1 - c), y) for d in (0, 1, 2, 3)]
    z_line = [(device((z + d) % 4, x, c), y) for d in (1, 2, 3)]
    z_other = [(device((z + d) % 4, x, 1 - c), y) for d in (1, 2, 3)]
    y_line = [(f, (y + d) % 4) for d in (1, 2, 3)]
    barrier = pltpu.get_barrier_semaphore()
    for peer in x_line + z_line + z_other + y_line:
        pl.semaphore_signal(barrier, inc=1, device_id=peer, device_id_type=MESH)
    blocks[64] = jnp.zeros((ROWS, ORDER), BF16)
    pl.semaphore_wait(barrier, 16)

    def send_grad(j):
        cc = (y + j) % 2

        def pack(n, carry):
            zz, xx = n // 4, n % 4
            piece = blocks[table[device(zz, xx, cc) * 3 + j]]
            packed[0, j, xx, zz] = piece[:, :512]
            packed[1, j, zz, xx] = piece[:, 512:]
            return carry

        lax.fori_loop(0, 16, pack, 0)
        for d in (1, 3, 2):
            xx, zz = (x + d) % 4, (z + d) % 4
            remote(packed.at[0, j, xx], passing.at[0, j, x], sem_g1s.at[j], sem_g1.at[j], device(z, xx, c), y).start()
            remote(packed.at[1, j, zz], passing.at[1, j, z], sem_g1s.at[j], sem_g1.at[j], device(zz, x, c), y).start()
        pltpu.make_async_copy(packed.at[0, j, x], passing.at[0, j, x], sem_g1.at[j]).start()
        pltpu.make_async_copy(packed.at[1, j, z], passing.at[1, j, z], sem_g1.at[j]).start()

    def relay_grad(j):
        cc = (y + j) % 2
        wait_units(16, sem_g1.at[j])
        for d in (1, 3, 2, 0):
            xx, zz = (x + d) % 4, (z + d) % 4
            move(passing.at[0, j, :, zz], whole.at[j, 0, z, :, c], sem_gs.at[j], sem_g.at[j], device(zz, x, cc))
            move(passing.at[1, j, :, xx], whole.at[j, 1, :, x, c], sem_gs.at[j], sem_g.at[j], device(z, xx, cc))

    def send_roots(j):
        def block(k, yy):
            at = roots.at[j * 16 + y * 4 + k]
            remote(at, at, sem_ls.at[j], sem_l.at[j], f, yy).start()

        @pl.when(does(j))
        def _():
            block(y, across)

        @pl.when(jnp.logical_not(does(j)))
        def _():
            for k in (y, up(j), across):
                block(k, down(j))
            for k in (y, down(j)):
                block(k, up(j))
            remote(rown.at[j], rnext.at[j], sem_rs.at[j], sem_r.at[j], f, down(j)).start()

    def fill(j):
        @pl.when(does(j))
        def _():
            wait_units(12, sem_l.at[j])
            u, d, a = up(j), down(j), across
            for r, k in ((u, y), (a, y), (d, y), (a, u), (d, u), (a, d)):
                roots[j * 16 + r * 4 + k] = roots[j * 16 + k * 4 + r].T

    def rows_at(j, h, r):
        return whole[j, h, r].reshape(SHARE, 512)

    def columns(j, root, out):
        def product(r, carry):
            value = lax.dot_general(rows_at(j, 0, r), root[j, :, :512], NT, preferred_element_type=F32)
            value += lax.dot_general(rows_at(j, 1, r), root[j, :, 512:], NT, preferred_element_type=F32)
            half[r] = value.astype(BF16)
            return carry

        lax.fori_loop(0, 4, product, 0)

        def outer(r, total):
            value = jnp.dot(roots[j * 16 + r * 4], half[0], preferred_element_type=F32)
            for k in range(1, 4):
                value += jnp.dot(roots[j * 16 + r * 4 + k], half[k], preferred_element_type=F32)
            part = jnp.sum(value * value, axis=0, keepdims=True)
            out[j, 0, r] = value[:, :128].astype(BF16).reshape(4, 2, ROWS, 128)
            out[j, 1, r] = value[:, 128:].astype(BF16).reshape(4, 2, ROWS, 128)
            return total + part[:, :128] + part[:, 128:]

        return lax.fori_loop(0, 4, outer, jnp.zeros((1, 128), F32))

    def send_part(j):
        for d in (1, 3, 2):
            xx, zz = (x + d) % 4, (z + d) % 4
            remote(mine.at[j, 0, :, xx], relayed.at[0, j, x], sem_s1s.at[j], sem_s1.at[j], device(z, xx, c), y).start()
            remote(mine.at[j, 1, zz], relayed.at[1, j, z], sem_s1s.at[j], sem_s1.at[j], device(zz, x, c), y).start()
        pltpu.make_async_copy(mine.at[j, 0, :, x], relayed.at[0, j, x], sem_s1.at[j]).start()
        pltpu.make_async_copy(mine.at[j, 1, z], relayed.at[1, j, z], sem_s1.at[j]).start()

    def relay_part(j):
        wait_units(8, sem_s1.at[j])
        for d in (1, 3, 2, 0):
            xx, zz = (x + d) % 4, (z + d) % 4
            for cc in (0, 1):
                move(relayed.at[0, j, :, zz, cc], got.at[0, j, z, :, c], sem_ss.at[j], sem_s, device(zz, x, cc))
                move(relayed.at[1, j, :, xx, cc], got.at[1, j, :, x, c], sem_ss.at[j], sem_s, device(z, xx, cc))

    def direct(j):
        @pl.when(does(j))
        def _():
            wait_units(8, sem_r.at[j])
            wait_units(32, sem_g.at[j])
            first = columns(j, rnext, give)
            remote(give.at[j], mine.at[j], sem_hs.at[j], sem_h.at[j], f, up(j)).start()
            other = columns(j, rown, mine)
            sham[pl.ds(f * 3 + j, 1), :] = first + other
            send_part(j)

    def take(j):
        @pl.when(jnp.logical_not(does(j)))
        def _():
            wait_units(8, sem_h.at[j])
            send_part(j)

    def statistics(j):
        @pl.when(does(j))
        def _():
            def left_rows(r):
                value = lax.dot_general(
                    rows_at(j, 0, r), whole[j, 0].reshape(ORDER, 512), NT, preferred_element_type=F32
                )
                value += lax.dot_general(
                    rows_at(j, 1, r), whole[j, 1].reshape(ORDER, 512), NT, preferred_element_type=F32
                )
                return value

            def right_rows(r):
                at = pl.ds(pl.multiple_of((r % 2) * SHARE, SHARE), SHARE)
                lhs = whole[j, r // 2, :, :, :, :, at].reshape(ORDER, SHARE).T
                return [
                    jnp.dot(lhs, whole[j, h].reshape(ORDER, 512), preferred_element_type=F32) for h in (0, 1)
                ]

            stat_out[j, 0] = left_rows(up(j)).astype(BF16)
            remote(stat_out.at[j, 0], stat_in.at[j, 0], sem_ps.at[j], sem_p.at[j], f, up(j)).start()
            for h, value in enumerate(right_rows(down(j))):
                stat_out[j, 1, :, h * 512 : (h + 1) * 512] = value.astype(BF16)
            remote(stat_out.at[j, 1], stat_in.at[j, 1], sem_qs.at[j], sem_q.at[j], f, down(j)).start()
            lstat[j] = 0.9 * lstat[j] + 0.1 * left_rows(y)
            for h, value in enumerate(right_rows(y)):
                at = slice(h * 512, (h + 1) * 512)
                rstat[j, :, at] = 0.9 * rstat[j, :, at] + 0.1 * value

    def receive(j):
        @pl.when(jnp.logical_not(does(j)))
        def _():
            wait_units(8, sem_p.at[j])
            lstat[j] = 0.9 * lstat[j] + 0.1 * stat_in[j, 0].astype(F32)
            wait_units(8, sem_q.at[j])
            rstat[j] = 0.9 * rstat[j] + 0.1 * stat_in[j, 1].astype(F32)

    stages = [x_line, z_line, y_line]

    def stage_copies(s):
        return [
            remote(tile.at[s], tiles_in.at[s, n], sem_ts.at[s, n], sem_t.at[s, n], *peer)
            for n, peer in enumerate(stages[s])
        ]

    def start_stage(s):
        for copy in stage_copies(s):
            copy.start()

    def end_stage(s):
        for copy in stage_copies(s):
            copy.wait()
        total = tile[s]
        for n in range(len(stages[s])):
            total += tiles_in[s, n]
        tile[s + 1] = total

    load_blocks.wait()
    send_grad(0)
    wait_units(24, sem_in.at[1])
    load_rown.wait()
    send_roots(0)
    send_roots(1)
    send_grad(1)
    send_roots(2)

    load_cols.wait()
    load_sec.wait()
    adam[...] = jnp.zeros_like(adam)
    sham[...] = jnp.zeros_like(sham)

    def adam_block(b, carry):
        wide = cols[b].astype(F32)
        new = 0.95 * sec[b] + 0.05 * wide * wide
        sec[b] = new
        value = wide / (jnp.sqrt(new) + 1e-08)
        part = jnp.sum(value * value, axis=0, keepdims=True)
        adam[pl.ds(b, 1), :] = part[:, :128] + part[:, 128:]
        return carry

    lax.fori_loop(0, 64, adam_block, 0)
    load_left.wait()
    load_right.wait()

    relay_grad(0)
    send_grad(2)
    relay_grad(1)
    fill(0)
    fill(1)
    direct(0)
    relay_grad(2)
    direct(1)
    take(0)
    statistics(0)
    relay_part(0)
    fill(2)
    take(1)
    statistics(1)
    direct(2)
    relay_part(1)
    take(2)
    tile[0] = jnp.zeros((8, 128), F32)
    tile[0, 0:1, :] = jnp.sum(adam[...].T, axis=0, keepdims=True)
    tile[0, 1:2, :] = jnp.sum(sham[...].T, axis=0, keepdims=True)
    start_stage(0)
    statistics(2)
    relay_part(2)
    end_stage(0)
    start_stage(1)
    receive(0)
    receive(1)
    end_stage(1)
    start_stage(2)
    receive(2)
    end_stage(2)
    store_sums = pltpu.make_async_copy(tile.at[3], sums_out, sem_in.at[0])
    store_sums.start()

    for j in range(3):
        wait_units(12, sem_g1s.at[j])
        wait_units(6, sem_s1s.at[j])
        wait_units(7, sem_ss.at[j])

        @pl.when(does(j))
        def _():
            wait_units(12, sem_gs.at[j])
            wait_units(2, sem_ls.at[j])
            wait_units(8, sem_hs.at[j])
            wait_units(8, sem_ps.at[j])
            wait_units(8, sem_qs.at[j])

        @pl.when(jnp.logical_not(does(j)))
        def _():
            wait_units(16, sem_gs.at[j])
            wait_units(8, sem_rs.at[j])
            wait_units(10, sem_ls.at[j])

    store_sums.wait()
    wait_units(24, sem_s)


def finish_kernel(slots, sums, lstat, rstat, sec, got, left_out, right_out, second_out, out, wide, sem):
    stores = []
    for n, (src, dst) in enumerate(((lstat, left_out), (rstat, right_out), (sec, second_out))):
        copy = pltpu.make_async_copy(src, dst, sem.at[n])
        copy.start()
        stores.append(copy)

    def one(b, carry):
        slot = slots[b]
        j, owner = slot % 3, slot // 3
        c, x, z = owner % 2, (owner // 2) % 4, owner // 8
        adam_sq = jnp.full((1, 128), sums[0, b], F32) * (1.0 / 1048576.0)
        sham_sq = jnp.full((1, 128), sums[1, slot], F32) * (1.0 / 1048576.0)
        factor = jnp.sqrt(adam_sq / (sham_sq + 1e-06))
        for h in (0, 1):
            wide[b, :, h * 128 : (h + 1) * 128] = got[h, j, z, x, c].astype(F32) * factor
        return carry

    for n in range(4):
        part = pl.ds(n * 16, 16)
        lax.fori_loop(n * 16, n * 16 + 16, one, 0)
        copy = pltpu.make_async_copy(wide.at[part], out.at[part], sem.at[3 + n])
        copy.start()
        stores.append(copy)
    for copy in stores:
        copy.wait()


def per_device(grad, second, left, right, left_root, right_root, slot_of_block):
    any_space, vmem = pl.BlockSpec(memory_space=pl.ANY), pl.BlockSpec(memory_space=pltpu.VMEM)
    smem = pl.BlockSpec(memory_space=pltpu.SMEM)
    slots = jnp.arange(96, dtype=jnp.int32)
    named = slot_of_block[None, :] == slots[:, None]
    table = jnp.min(jnp.where(named, jnp.arange(64, dtype=jnp.int32)[None, :], 64), axis=1)
    dma = pltpu.SemaphoreType.DMA
    lstat, rstat, sec, got, sums = pl.pallas_call(
        exchange_kernel,
        name="exchange",
        out_shape=(
            pltpu.VMEM((3, 256, 1024), F32),
            pltpu.VMEM((3, 256, 1024), F32),
            pltpu.VMEM((64, 32, 256), F32),
            pltpu.VMEM((2, 3, 4, 4, 2, 32, 128), BF16),
            jax.ShapeDtypeStruct((8, 128), F32),
        ),
        in_specs=[smem] + [any_space] * 6,
        out_specs=(vmem,) * 4 + (any_space,),
        scratch_shapes=[
            pltpu.VMEM((65, 32, 1024), BF16),
            pltpu.VMEM((64, 32, 256), BF16),
            pltpu.VMEM((2, 3, 4, 4, 32, 512), BF16),
            pltpu.VMEM((2, 3, 4, 4, 32, 512), BF16),
            pltpu.VMEM((3, 2, 4, 4, 2, 32, 512), BF16),
            pltpu.VMEM((48, 256, 256), BF16),
            pltpu.VMEM((3, 256, 1024), BF16),
            pltpu.VMEM((3, 256, 1024), BF16),
            pltpu.VMEM((4, 256, 256), BF16),
            pltpu.VMEM((3, 2, 4, 4, 2, 32, 128), BF16),
            pltpu.VMEM((3, 2, 4, 4, 2, 32, 128), BF16),
            pltpu.VMEM((2, 3, 4, 4, 2, 32, 128), BF16),
            pltpu.VMEM((3, 2, 256, 1024), BF16),
            pltpu.VMEM((3, 2, 256, 1024), BF16),
            pltpu.VMEM((128, 128), F32),
            pltpu.VMEM((128, 128), F32),
            pltpu.VMEM((4, 8, 128), F32),
            pltpu.VMEM((3, 7, 8, 128), F32),
            dma((7,)),
            dma((3,)), dma((3,)),
            dma((3,)), dma((3,)),
            dma((3,)), dma((3,)),
            dma((3,)), dma((3,)),
            dma((3,)), dma((3,)),
            dma((3,)), dma((3,)),
            dma, dma((3,)),
            dma((3,)), dma((3,)),
            dma((3,)), dma((3,)),
            dma((3, 7)), dma((3, 7)),
        ],
        compiler_params=pltpu.CompilerParams(
            collective_id=0, has_side_effects=True, vmem_limit_bytes=EXCHANGE_VMEM
        ),
    )(table, grad, second, left, right, left_root, right_root)
    return pl.pallas_call(
        finish_kernel,
        name="finish",
        out_shape=(
            jax.ShapeDtypeStruct((3, 256, 1024), F32),
            jax.ShapeDtypeStruct((3, 256, 1024), F32),
            jax.ShapeDtypeStruct((64, 32, 256), F32),
            jax.ShapeDtypeStruct((64, 32, 256), F32),
        ),
        in_specs=[smem, smem] + [vmem] * 4,
        out_specs=(any_space,) * 4,
        scratch_shapes=[pltpu.VMEM((64, 32, 256), F32), dma((7,))],
        compiler_params=pltpu.CompilerParams(vmem_limit_bytes=FINISH_VMEM),
    )(slot_of_block, sums, lstat, rstat, sec, got)


def solution(mesh):
    return jax.shard_map(
        per_device,
        mesh=mesh,
        in_specs=(
            P(None, "fsdp", None),
            P(None, "fsdp", "grp"),
            P("fsdp", "grp", None),
            P("fsdp", "grp", None),
            P("fsdp", "grp", None),
            P("fsdp", "grp", None),
            P(),
        ),
        out_specs=(
            P("fsdp", "grp", None),
            P("fsdp", "grp", None),
            P(None, "fsdp", "grp"),
            P(None, "fsdp", "grp"),
        ),
        check_vma=False,
    )
```

time: 275 us -> 87.8 us (0.32)
  blocking collectives: 134 us -> 0 us
  Pallas kernels: 0 us -> 84.4 us
  waiting for transfers between devices: 35.8 us -> 0 us
  local copies, waits for them, and re-layouts: 36.1 us -> 0.67 us
  matrix products: 24.9 us -> 0 us
  starting transfers between devices: 17.1 us -> 0 us
  between operations: 14.1 us -> 0.66 us
  other arithmetic: 9.51 us -> 1.26 us
    psum x2 -> x0, blocking collectives: 134 us -> none  [the longest x1 126 us: per_device(): adam_total = lax.psum(adam_part, ('fsdp', 'grp'))]
    pallas_call x0 -> x2, Pallas kernels: none -> 84.4 us  [the longest x1 79.8 us: per_device(): pl.pallas_call(exchange_kernel, name='exchange', out_shape=(pltpu.VMEM((3...]
    all_to_all x2 -> x0, waiting for transfers between devices: 35.1 us -> none  [the longest x1 35.1 us: per_device(): lax.all_to_all(outgoing, 'fsdp', split_axis=1, concat_axis=0, tiled=True)]
    dot_general x3 -> x0, matrix products: 24.9 us -> none  [the longest x1 9.77 us: per_device(): jnp.einsum('srk,skc->src', lax.all_gather(left_root, 'grp', axis=1, tiled...]
    all_to_all x2 -> x0, starting transfers between devices: 17.1 us -> none  [the longest x1 9.61 us: per_device(): lax.all_to_all(packed, 'fsdp', split_axis=0, concat_axis=1, tiled=True)]
    scatter x1 -> x0, local copies, waits for them, and re-layouts: 12.2 us -> none  [per_device(): jnp.zeros((total_slots, rows_here, order), jnp.bfloat16).at[slot_of_block]]
    all_to_all x3 -> x0, local copies, waits for them, and re-layouts: 11.5 us -> none  [the longest x1 6.77 us: per_device(): lax.all_to_all(packed, 'fsdp', split_axis=0, concat_axis=1, tiled=True)]
    mul x1 -> x0, local copies, waits for them, and re-layouts: 5.05 us -> none  [per_device(): outgoing = shampoo_columns * slot_factor[:, None, None]]
  transfers between devices with their start and end apart: 3 -> 0, of which waited for: 1 -> 0; matrix products, arithmetic and copies ran while one was open for 16% -> 0% of each run, Pallas kernels for 0% -> 0%
where the time goes in v2:
time: 87.8 us; the launch traced here: 87 us
  Pallas kernels  84.4 us (96%)
  other arithmetic  1.26 us (1%)
    pallas_call x1, Pallas kernels, per_device(): pl.pallas_call(exchange_kernel, name='exchange', out_shape=(pltpu.VMEM((3...  79.8 us
    pallas_call x1, Pallas kernels, per_device(): pl.pallas_call(finish_kernel, name='finish', out_shape=(jax.ShapeDtypeStr...  4.63 us

profile of v2, /device:TPU:1, one launch (start us, length us, event | category | flops | bytes accessed | tf_op | source)
XLA Modules:
  0.0 87.0 jit_solution(7458121742146901427)
XLA Ops:
  0.6 1.3 %select_reduce_fusion.table = s32[96]{0:T(128)} fusion(s32[64]{0:T(128)} %slots.1), kind=kLoop, calls=%fused_computation | loop fusion | flops 18336 | bytes 640 | tf_op jit(solution)/shard_map/reduce_min | solution.py:365
  1.9 0.0 copy-start.1
  1.9 79.8 %exchange.1 = (f32[3,256,1024]{2,1,0:T(8,128)S(1)}, f32[3,256,1024]{2,1,0:T(8,128)S(1)}, f32[64,32,256]{2,1,0:T(8,128)S(1)}, bf16[2,3,4,4,2,32,128]{6,5,4,3,2,1,0:T(8,128)(2,1)S(1)}, f32[8,128]{1,0:T(8,128)}) custom-call(s32[96]{0:T(128)} %select_reduce_fusion.table, bf16[64,32,1024]{2,1,0:T(8,128)(2,1)} %grad.1, f32[64,32,256]{2,1,0:T(8,128)} %second.1, ...), custom_call_target="tpu_custom_call" | custom-call | tf_op jit(solution)/shard_map/exchange/pallas_call | solution.py:367
  81.7 0.0 copy-done.1
  81.7 0.0 copy-start
  81.7 0.7 copy-done
  82.4 4.6 %finish.1 = (f32[3,256,1024]{2,1,0:T(8,128)}, f32[3,256,1024]{2,1,0:T(8,128)}, f32[64,32,256]{2,1,0:T(8,128)}, f32[64,32,256]{2,1,0:T(8,128)}) custom-call(s32[64]{0:T(128)S(1)} %copy-done.1, f32[8,128]{1,0:T(8,128)S(1)} %copy-done, f32[3,256,1024]{2,1,0:T(8,128)S(1)} %get-tuple-element.10.lstat, f32[3,256,1024]{2,1,0:T(8,128)S(1)} %get-tuple-element.11.rstat, ...), custom_call_target="tpu_custom_call" | custom-call | tf_op jit(solution)/shard_map/finish/pallas_call | solution.py:414
Async XLA Ops:
  1.9 79.8 %copy-start.1 = (s32[64]{0:T(128)S(1)}, s32[64]{0:T(128)}, u32[]{:S(2)}) copy-start(s32[64]{0:T(128)} %slots.1) | copy-start | bytes 772
  81.7 0.7 copy-start

commit v3 on v2

v3 whole, which is shorter than its diff:
```python
import jax
import jax.numpy as jnp
from jax import lax
from jax.experimental import pallas as pl
from jax.experimental.pallas import tpu as pltpu
from jax.sharding import PartitionSpec as P

MESH = pl.DeviceIdType.MESH
F32, BF16 = jnp.float32, jnp.bfloat16
NT = (((1,), (1,)), ((), ()))
EXCHANGE_VMEM = 50 * 2**20
FINISH_VMEM = 16 * 2**20
SHARE, ROWS, ORDER = 256, 32, 1024


def exchange_kernel(
    table, grad, second, left, right, left_root, right_root,
    lstat, rstat, sec, got, sums_out,
    blocks, cols, packed, passing, whole, roots, rown, rnext, half,
    mine, give, relayed, stat_out, stat_in, adam, sham, tile, tiles_in,
    sem_in, sem_g1, sem_g1s, sem_g, sem_gs, sem_l, sem_ls, sem_r, sem_rs,
    sem_os, sem_hs, sem_s1, sem_s1s, sem_s, sem_ss, sem_p, sem_ps, sem_q, sem_qs, sem_t, sem_ts,
):
    f, y = lax.axis_index("fsdp"), lax.axis_index("grp")
    c, x, z = f % 2, (f // 2) % 4, f // 8
    up, down, across = (y + 1 + 2 * c) % 4, (y + 3 + 2 * c) % 4, (y + 2) % 4

    def device(zz, xx, cc):
        return zz * 8 + xx * 2 + cc


    def remote(src, dst, send, recv, ff, yy):
        return pltpu.make_async_remote_copy(
            src_ref=src, dst_ref=dst, send_sem=send, recv_sem=recv, device_id=(ff, yy), device_id_type=MESH
        )

    def move(src, dst, send, recv, ff):
        @pl.when(ff == f)
        def _():
            pltpu.make_async_copy(src, dst, recv).start()

        @pl.when(ff != f)
        def _():
            remote(src, dst, send, recv, ff, y).start()

    def wait_bytes(ref, sem):
        pltpu.make_async_copy(ref, ref, sem).wait()

    def wait_units(n, sem):
        wait_bytes(blocks.at[pl.ds(0, n)], sem)

    def load(src, dst, n):
        copy = pltpu.make_async_copy(src, dst, sem_in.at[n])
        copy.start()
        return copy

    load_blocks = load(grad, blocks.at[pl.ds(0, 64)], 0)
    for j in range(3):
        for k in range(4):
            load(left_root.at[j, :, pl.ds(k * SHARE, SHARE)], roots.at[j * 16 + k * 4 + y], 1)
            load(right_root.at[j, :, pl.ds(k * SHARE, SHARE)], rown.at[j * 4 + k], 2)
    load_cols = load(grad.at[:, :, pl.ds(pl.multiple_of(y * SHARE, SHARE), SHARE)], cols, 3)
    load_sec = load(second, sec, 4)
    load_left = load(left, lstat, 5)
    load_right = load(right, rstat, 6)

    x_line = [(device(z, (x + d) % 4, c), y) for d in (1, 2, 3)]
    x_line += [(device(z, (x + d) % 4, 1 - c), y) for d in (0, 1, 2, 3)]
    z_line = [(device((z + d) % 4, x, c), y) for d in (1, 2, 3)]
    z_other = [(device((z + d) % 4, x, 1 - c), y) for d in (1, 2, 3)]
    y_line = [(f, (y + d) % 4) for d in (1, 2, 3)]
    senders = x_line + z_line + z_other + y_line
    for cc, yy in ((0, (y + 3) % 4), (1, (y + 1) % 4)):
        senders += [(device(z, (x + d) % 4, cc), yy) for d in (0, 1, 2, 3)]
        senders += [(device((z + d) % 4, x, cc), yy) for d in (1, 2, 3)]
    barrier = pltpu.get_barrier_semaphore()
    for peer in senders:
        pl.semaphore_signal(barrier, inc=1, device_id=peer, device_id_type=MESH)
    blocks[64] = jnp.zeros((ROWS, ORDER), BF16)
    pl.semaphore_wait(barrier, 30)

    def to_handler(j, route, piece, zs, xs, other):
        cc = (y + j) % 2
        ff = device(other, x, cc) if route == 0 else device(z, other, cc)
        move(piece, whole.at[j, route, zs, xs, c], sem_gs.at[j], sem_g.at[j], ff)

    def send_grad(j):
        cc = (y + j) % 2

        def pack(n, carry):
            zz, xx = n // 4, n % 4
            piece = blocks[table[device(zz, xx, cc) * 3 + j]]
            packed[0, j, xx, zz] = piece[:, :512]
            packed[1, j, zz, xx] = piece[:, 512:]
            return carry

        lax.fori_loop(0, 16, pack, 0)
        for d in (1, 3, 2):
            xx, zz = (x + d) % 4, (z + d) % 4
            remote(
                packed.at[0, j, xx], passing.at[0, j, x], sem_g1s.at[j], sem_g1.at[0, j, x], device(z, xx, c), y
            ).start()
            remote(
                packed.at[1, j, zz], passing.at[1, j, z], sem_g1s.at[j], sem_g1.at[1, j, z], device(zz, x, c), y
            ).start()
        for d in (1, 3, 2, 0):
            xx, zz = (x + d) % 4, (z + d) % 4
            to_handler(j, 0, packed.at[0, j, x, zz], z, x, zz)
            to_handler(j, 1, packed.at[1, j, z, xx], z, x, xx)

    def relay_grad(j):
        for e in (1, 3, 2):
            xs, zs = (x + e) % 4, (z + e) % 4
            wait_units(2, sem_g1.at[0, j, xs])
            for d in (1, 3, 2, 0):
                to_handler(j, 0, passing.at[0, j, xs, (z + d) % 4], z, xs, (z + d) % 4)
            wait_units(2, sem_g1.at[1, j, zs])
            for d in (1, 3, 2, 0):
                to_handler(j, 1, passing.at[1, j, zs, (x + d) % 4], zs, x, (x + d) % 4)

    def send_roots(j, handled):
        def block(k, yy):
            at = roots.at[j * 16 + k * 4 + y]
            remote(at, at, sem_ls.at[j], sem_l.at[j], f, yy).start()

        if handled:
            block(y, across)
        else:
            for k in (y, up, across):
                block(k, down)
                at = j * 4 + k
                remote(rown.at[at], rnext.at[at], sem_rs.at[j], sem_r.at[j], f, down).start()
            for k in (y, down):
                block(k, up)

    def fill(j):
        wait_units(12, sem_l.at[j])
        for r, k in ((up, y), (across, y), (down, y), (across, up), (down, up), (across, down)):
            roots[j * 16 + k * 4 + r] = roots[j * 16 + r * 4 + k].T
        rnext[j * 4 + y] = rown[j * 4 + up].T

    def rows_at(j, h, r):
        return whole[j, h, r].reshape(SHARE, 512)

    def direct(j):
        wait_units(6, sem_r.at[j])
        wait_units(32, sem_g.at[j])
        lhs = jnp.concatenate([whole[j, h].reshape(ORDER, 512) for h in (0, 1)], axis=1)
        rhs = jnp.concatenate(
            [jnp.concatenate([root[j * 4 + k] for k in range(4)], axis=1) for root in (rnext, rown)], axis=0
        )
        half[...] = lax.dot_general(lhs, rhs, NT, preferred_element_type=F32).astype(BF16)
        lhs = jnp.concatenate(
            [roots[j * 16 + k * 4 : j * 16 + k * 4 + 4].reshape(ORDER, SHARE) for k in range(4)], axis=1
        )
        value = jnp.dot(lhs, half[...], preferred_element_type=F32)
        for n, out in enumerate((give, mine)):
            for h in (0, 1):
                at = n * SHARE + h * 128
                out[j, h] = value[:, at : at + 128].astype(BF16).reshape(4, 4, 2, ROWS, 128)
        part = jnp.sum(value * value, axis=0, keepdims=True)
        sham[pl.ds(f * 3 + j, 1), :] = part[:, :128] + part[:, 128:256] + part[:, 256:384] + part[:, 384:]

    def send_part(j):
        for d in (1, 3, 2):
            xx, zz = (x + d) % 4, (z + d) % 4
            for src, yy in ((give, up), (mine, y)):
                remote(
                    src.at[j, 0, :, xx], relayed.at[0, j, 4 - d], sem_s1s.at[j], sem_s1.at[0, j], device(z, xx, c), yy
                ).start()
                remote(
                    src.at[j, 1, zz], relayed.at[1, j, 4 - d], sem_s1s.at[j], sem_s1.at[1, j], device(zz, x, c), yy
                ).start()
        for d in (1, 3, 2, 0):
            xx, zz = (x + d) % 4, (z + d) % 4
            for cc in (0, 1):
                remote(
                    give.at[j, 0, zz, x, cc], got.at[0, j, z, 0, c], sem_hs.at[j], sem_s, device(zz, x, cc), up
                ).start()
                remote(
                    give.at[j, 1, z, xx, cc], got.at[1, j, x, 0, c], sem_hs.at[j], sem_s, device(z, xx, cc), up
                ).start()
                move(mine.at[j, 0, zz, x, cc], got.at[0, j, z, 0, c], sem_os.at[j], sem_s, device(zz, x, cc))
                move(mine.at[j, 1, z, xx, cc], got.at[1, j, x, 0, c], sem_os.at[j], sem_s, device(z, xx, cc))

    def relay_part(j):
        others = pl.ds(1, 3)
        wait_units(3, sem_s1.at[0, j])
        for d in (1, 3, 2, 0):
            zz = (z + d) % 4
            for cc in (0, 1):
                move(
                    relayed.at[0, j, others, zz, cc], got.at[0, j, z, others, c], sem_ss.at[j], sem_s,
                    device(zz, x, cc),
                )
        wait_units(3, sem_s1.at[1, j])
        for d in (1, 3, 2, 0):
            xx = (x + d) % 4
            for cc in (0, 1):
                move(
                    relayed.at[1, j, others, xx, cc], got.at[1, j, x, others, c], sem_ss.at[j], sem_s,
                    device(z, xx, cc),
                )

    def left_rows(j, r):
        value = lax.dot_general(rows_at(j, 0, r), whole[j, 0].reshape(ORDER, 512), NT, preferred_element_type=F32)
        value += lax.dot_general(rows_at(j, 1, r), whole[j, 1].reshape(ORDER, 512), NT, preferred_element_type=F32)
        return value

    def right_rows(j, r):
        at = pl.ds(pl.multiple_of((r % 2) * SHARE, SHARE), SHARE)
        lhs = whole[j, r // 2, :, :, :, :, at].reshape(ORDER, SHARE).T
        return [jnp.dot(lhs, whole[j, h].reshape(ORDER, 512), preferred_element_type=F32) for h in (0, 1)]

    def next_left(j):
        stat_out[j, 0] = left_rows(j, up).astype(BF16)
        remote(stat_out.at[j, 0], stat_in.at[j, 0], sem_ps.at[j], sem_p.at[j], f, up).start()

    def next_right(j):
        for h, value in enumerate(right_rows(j, down)):
            stat_out[j, 1, :, h * 512 : (h + 1) * 512] = value.astype(BF16)
        remote(stat_out.at[j, 1], stat_in.at[j, 1], sem_qs.at[j], sem_q.at[j], f, down).start()

    def own_left(j):
        lstat[j] = 0.9 * lstat[j] + 0.1 * left_rows(j, y)

    def own_right(j):
        for h, value in enumerate(right_rows(j, y)):
            at = slice(h * 512, (h + 1) * 512)
            rstat[j, :, at] = 0.9 * rstat[j, :, at] + 0.1 * value

    def receive_left(j):
        wait_units(8, sem_p.at[j])
        lstat[j] = 0.9 * lstat[j] + 0.1 * stat_in[j, 0].astype(F32)

    def receive_right(j):
        wait_units(8, sem_q.at[j])
        rstat[j] = 0.9 * rstat[j] + 0.1 * stat_in[j, 1].astype(F32)

    stages = [x_line, z_line, y_line]

    def stage_copies(s):
        return [
            remote(tile.at[s], tiles_in.at[s, n], sem_ts.at[s, n], sem_t.at[s, n], *peer)
            for n, peer in enumerate(stages[s])
        ]

    def start_stage(s):
        for copy in stage_copies(s):
            copy.start()

    def end_stage(s):
        for copy in stage_copies(s):
            copy.wait()
        total = tile[s]
        for n in range(len(stages[s])):
            total += tiles_in[s, n]
        tile[s + 1] = total

    def start_sums():
        tile[0] = jnp.zeros((8, 128), F32)
        tile[0, 0:1, :] = jnp.sum(adam[...].T, axis=0, keepdims=True)
        tile[0, 1:2, :] = jnp.sum(sham[...].T, axis=0, keepdims=True)
        start_stage(0)

    def wait_sent(handled):
        for j in range(3):
            wait_units(12, sem_g1s.at[j])
            wait_bytes(blocks.at[pl.ds(0, 21), pl.ds(0, 16), pl.ds(0, 512)], sem_ss.at[j])
            if j in handled:
                wait_units(12, sem_s1s.at[j])
                wait_units(2, sem_hs.at[j])
                wait_bytes(blocks.at[pl.ds(0, 7), pl.ds(0, 16), pl.ds(0, 512)], sem_os.at[j])
                wait_units(12, sem_gs.at[j])
                wait_units(2, sem_ls.at[j])
                wait_units(8, sem_ps.at[j])
                wait_units(8, sem_qs.at[j])
            else:
                wait_units(16, sem_gs.at[j])
                wait_units(6, sem_rs.at[j])
                wait_units(10, sem_ls.at[j])

    load_blocks.wait()
    send_grad(0)
    wait_units(24, sem_in.at[1])
    wait_units(24, sem_in.at[2])

    @pl.when((y + c) % 2 == 0)
    def _():
        send_roots(0, True)
        send_roots(1, False)
        send_roots(2, True)

    @pl.when((y + c) % 2 == 1)
    def _():
        send_roots(0, False)
        send_roots(1, True)

    load_cols.wait()
    load_sec.wait()
    adam[...] = jnp.zeros_like(adam)
    sham[...] = jnp.zeros_like(sham)

    def adam_block(b, carry):
        wide = cols[b].astype(F32)
        new = 0.95 * sec[b] + 0.05 * wide * wide
        sec[b] = new
        value = wide / (jnp.sqrt(new) + 1e-08)
        part = jnp.sum(value * value, axis=0, keepdims=True)
        adam[pl.ds(b, 1), :] = part[:, :128] + part[:, 128:]
        return carry

    lax.fori_loop(0, 64, adam_block, 0)
    load_left.wait()
    load_right.wait()
    relay_grad(0)

    @pl.when((y + c) % 2 == 0)
    def _():
        send_grad(1)
        fill(0)
        relay_grad(1)
        send_grad(2)
        direct(0)
        next_left(0)
        next_right(0)
        own_left(0)
        own_right(0)
        fill(2)
        relay_grad(2)
        send_part(0)
        direct(2)
        send_part(2)
        start_sums()
        relay_part(0)
        next_right(2)
        next_left(2)
        relay_part(1)
        end_stage(0)
        start_stage(1)
        own_left(2)
        own_right(2)
        end_stage(1)
        start_stage(2)
        receive_left(1)
        receive_right(1)
        relay_part(2)
        end_stage(2)
        wait_sent((0, 2))

    @pl.when((y + c) % 2 == 1)
    def _():
        send_grad(1)
        send_roots(2, False)
        fill(1)
        relay_grad(1)
        send_grad(2)
        relay_grad(2)
        direct(1)
        send_part(1)
        next_left(1)
        next_right(1)
        start_sums()
        relay_part(0)
        own_left(1)
        own_right(1)
        relay_part(1)
        end_stage(0)
        start_stage(1)
        receive_left(0)
        receive_right(0)
        end_stage(1)
        start_stage(2)
        relay_part(2)
        receive_left(2)
        receive_right(2)
        end_stage(2)
        wait_sent((1,))

    sums_out[...] = tile[3]
    wait_units(24, sem_s)


def finish_kernel(slots, lstat, rstat, sec, got, sums, left_out, right_out, second_out, out, wide, rows, sem):
    stores = []
    for n, (src, dst) in enumerate(((lstat, left_out), (rstat, right_out), (sec, second_out))):
        copy = pltpu.make_async_copy(src, dst, sem.at[n])
        copy.start()
        stores.append(copy)

    f = lax.axis_index("fsdp")
    x, z = (f // 2) % 4, f // 8
    for n in (0, 1):
        rows[n] = jnp.broadcast_to(sums[n : n + 1, :], (128, 128)).T

    def one(b, carry):
        slot = slots[b]
        j, owner = slot % 3, slot // 3
        c, xs, zs = owner % 2, (owner // 2) % 4, owner // 8
        adam_sq = rows[0, pl.ds(b, 1), :] * (1.0 / 1048576.0)
        sham_sq = rows[1, pl.ds(slot, 1), :] * (1.0 / 1048576.0)
        factor = jnp.sqrt(adam_sq / (sham_sq + 1e-06))
        wide[b, :, :128] = got[0, j, zs, (xs + 4 - x) % 4, c].astype(F32) * factor
        wide[b, :, 128:] = got[1, j, xs, (zs + 4 - z) % 4, c].astype(F32) * factor
        return carry

    for n in range(4):
        part = pl.ds(n * 16, 16)
        lax.fori_loop(n * 16, n * 16 + 16, one, 0)
        copy = pltpu.make_async_copy(wide.at[part], out.at[part], sem.at[3 + n])
        copy.start()
        stores.append(copy)
    for copy in stores:
        copy.wait()


def per_device(grad, second, left, right, left_root, right_root, slot_of_block):
    any_space, vmem = pl.BlockSpec(memory_space=pl.ANY), pl.BlockSpec(memory_space=pltpu.VMEM)
    smem = pl.BlockSpec(memory_space=pltpu.SMEM)
    slots = jnp.arange(96, dtype=jnp.int32)
    named = slot_of_block[None, :] == slots[:, None]
    table = jnp.min(jnp.where(named, jnp.arange(64, dtype=jnp.int32)[None, :], 64), axis=1)
    dma = pltpu.SemaphoreType.DMA
    lstat, rstat, sec, got, sums = pl.pallas_call(
        exchange_kernel,
        name="exchange",
        out_shape=(
            pltpu.VMEM((3, 256, 1024), F32),
            pltpu.VMEM((3, 256, 1024), F32),
            pltpu.VMEM((64, 32, 256), F32),
            pltpu.VMEM((2, 3, 4, 4, 2, 32, 128), BF16),
            pltpu.VMEM((8, 128), F32),
        ),
        in_specs=[smem] + [any_space] * 6,
        out_specs=(vmem,) * 5,
        scratch_shapes=[
            pltpu.VMEM((65, 32, 1024), BF16),
            pltpu.VMEM((64, 32, 256), BF16),
            pltpu.VMEM((2, 3, 4, 4, 32, 512), BF16),
            pltpu.VMEM((2, 3, 4, 4, 32, 512), BF16),
            pltpu.VMEM((3, 2, 4, 4, 2, 32, 512), BF16),
            pltpu.VMEM((48, 256, 256), BF16),
            pltpu.VMEM((12, 256, 256), BF16),
            pltpu.VMEM((12, 256, 256), BF16),
            pltpu.VMEM((1024, 512), BF16),
            pltpu.VMEM((3, 2, 4, 4, 2, 32, 128), BF16),
            pltpu.VMEM((3, 2, 4, 4, 2, 32, 128), BF16),
            pltpu.VMEM((2, 3, 4, 4, 2, 32, 128), BF16),
            pltpu.VMEM((3, 2, 256, 1024), BF16),
            pltpu.VMEM((3, 2, 256, 1024), BF16),
            pltpu.VMEM((128, 128), F32),
            pltpu.VMEM((128, 128), F32),
            pltpu.VMEM((4, 8, 128), F32),
            pltpu.VMEM((3, 7, 8, 128), F32),
            dma((7,)),
            dma((2, 3, 4)), dma((3,)),
            dma((3,)), dma((3,)),
            dma((3,)), dma((3,)),
            dma((3,)), dma((3,)),
            dma((3,)), dma((3,)),
            dma((2, 3)), dma((3,)),
            dma, dma((3,)),
            dma((3,)), dma((3,)),
            dma((3,)), dma((3,)),
            dma((3, 7)), dma((3, 7)),
        ],
        compiler_params=pltpu.CompilerParams(
            collective_id=0, has_side_effects=True, vmem_limit_bytes=EXCHANGE_VMEM
        ),
    )(table, grad, second, left, right, left_root, right_root)
    return pl.pallas_call(
        finish_kernel,
        name="finish",
        out_shape=(
            jax.ShapeDtypeStruct((3, 256, 1024), F32),
            jax.ShapeDtypeStruct((3, 256, 1024), F32),
            jax.ShapeDtypeStruct((64, 32, 256), F32),
            jax.ShapeDtypeStruct((64, 32, 256), F32),
        ),
        in_specs=[smem] + [vmem] * 5,
        out_specs=(any_space,) * 4,
        scratch_shapes=[pltpu.VMEM((64, 32, 256), F32), pltpu.VMEM((2, 128, 128), F32), dma((7,))],
        compiler_params=pltpu.CompilerParams(vmem_limit_bytes=FINISH_VMEM),
    )(slot_of_block, lstat, rstat, sec, got, sums)


def solution(mesh):
    return jax.shard_map(
        per_device,
        mesh=mesh,
        in_specs=(
            P(None, "fsdp", None),
            P(None, "fsdp", "grp"),
            P("fsdp", "grp", None),
            P("fsdp", "grp", None),
            P("fsdp", "grp", None),
            P("fsdp", "grp", None),
            P(),
        ),
        out_specs=(
            P("fsdp", "grp", None),
            P("fsdp", "grp", None),
            P(None, "fsdp", "grp"),
            P(None, "fsdp", "grp"),
        ),
        check_vma=False,
    )
```

time: 87.8 us -> 75.4 us (0.86)
  Pallas kernels: 84.4 us -> 73.2 us
    pallas_call x1, Pallas kernels: 79.8 us -> 68.6 us  [per_device(): pl.pallas_call(exchange_kernel, name='exchange', out_shape=(pltpu.VMEM((3...]
where the time goes in v3:
time: 75.4 us; the launch traced here: 75.3 us
  Pallas kernels  73.2 us (97%)
  other arithmetic  1.26 us (2%)
  between operations  0.83 us (1%)
    pallas_call x1, Pallas kernels, per_device(): pl.pallas_call(exchange_kernel, name='exchange', out_shape=(pltpu.VMEM((3...  68.6 us
    pallas_call x1, Pallas kernels, per_device(): pl.pallas_call(finish_kernel, name='finish', out_shape=(jax.ShapeDtypeStr...  4.58 us

profile of v3, /device:TPU:1, one launch (start us, length us, event | category | flops | bytes accessed | tf_op | source)
XLA Modules:
  0.0 75.3 jit_solution(3205188213097788768)
XLA Ops:
  0.6 1.3 %select_reduce_fusion.table = s32[96]{0:T(128)} fusion(s32[64]{0:T(128)} %slots.1), kind=kLoop, calls=%fused_computation | loop fusion | flops 18336 | bytes 640 | tf_op jit(solution)/shard_map/reduce_min | solution.py:422
  1.9 0.0 copy-start
  1.9 68.6 %exchange.1 = (f32[3,256,1024]{2,1,0:T(8,128)S(1)}, f32[3,256,1024]{2,1,0:T(8,128)S(1)}, f32[64,32,256]{2,1,0:T(8,128)S(1)}, bf16[2,3,4,4,2,32,128]{6,5,4,3,2,1,0:T(8,128)(2,1)S(1)}, f32[8,128]{1,0:T(8,128)S(1)}) custom-call(s32[96]{0:T(128)} %select_reduce_fusion.table, bf16[64,32,1024]{2,1,0:T(8,128)(2,1)} %grad.1, f32[64,32,256]{2,1,0:T(8,128)} %second.1, ...), custom_call_target="tpu_custom_call" | custom-call | tf_op jit(solution)/shard_map/exchange/pallas_call | solution.py:424
  70.5 0.0 copy-done
  70.5 4.6 %finish.1 = (f32[3,256,1024]{2,1,0:T(8,128)}, f32[3,256,1024]{2,1,0:T(8,128)}, f32[64,32,256]{2,1,0:T(8,128)}, f32[64,32,256]{2,1,0:T(8,128)}) custom-call(s32[64]{0:T(128)S(1)} %copy-done, f32[3,256,1024]{2,1,0:T(8,128)S(1)} %get-tuple-element.9.lstat, f32[3,256,1024]{2,1,0:T(8,128)S(1)} %get-tuple-element.10.rstat, ...), custom_call_target="tpu_custom_call" | custom-call | tf_op jit(solution)/shard_map/finish/pallas_call | solution.py:471
Async XLA Ops:
  1.9 68.6 %copy-start = (s32[64]{0:T(128)S(1)}, s32[64]{0:T(128)}, u32[]{:S(2)}) copy-start(s32[64]{0:T(128)} %slots.1) | copy-start | bytes 772

commit v4 on v3

--- a/solution.py
+++ b/solution.py
@@ -14,9 +14,9 @@
 
 
 def exchange_kernel(
-    table, grad, second, left, right, left_root, right_root,
+    slots, grad, second, left, right, left_root, right_root,
     lstat, rstat, sec, got, sums_out,
-    blocks, cols, packed, passing, whole, roots, rown, rnext, half,
+    table, ranks, blocks, cols, packed, passing, whole, roots, rown, rnext, half,
     mine, give, relayed, stat_out, stat_in, adam, sham, tile, tiles_in,
     sem_in, sem_g1, sem_g1s, sem_g, sem_gs, sem_l, sem_ls, sem_r, sem_rs,
     sem_os, sem_hs, sem_s1, sem_s1s, sem_s, sem_ss, sem_p, sem_ps, sem_q, sem_qs, sem_t, sem_ts,
@@ -48,21 +48,6 @@
 
     def wait_units(n, sem):
         wait_bytes(blocks.at[pl.ds(0, n)], sem)
-
-    def load(src, dst, n):
-        copy = pltpu.make_async_copy(src, dst, sem_in.at[n])
-        copy.start()
-        return copy
-
-    load_blocks = load(grad, blocks.at[pl.ds(0, 64)], 0)
-    for j in range(3):
-        for k in range(4):
-            load(left_root.at[j, :, pl.ds(k * SHARE, SHARE)], roots.at[j * 16 + k * 4 + y], 1)
-            load(right_root.at[j, :, pl.ds(k * SHARE, SHARE)], rown.at[j * 4 + k], 2)
-    load_cols = load(grad.at[:, :, pl.ds(pl.multiple_of(y * SHARE, SHARE), SHARE)], cols, 3)
-    load_sec = load(second, sec, 4)
-    load_left = load(left, lstat, 5)
-    load_right = load(right, rstat, 6)
 
     x_line = [(device(z, (x + d) % 4, c), y) for d in (1, 2, 3)]
     x_line += [(device(z, (x + d) % 4, 1 - c), y) for d in (0, 1, 2, 3)]
@@ -76,25 +61,50 @@
     barrier = pltpu.get_barrier_semaphore()
     for peer in senders:
         pl.semaphore_signal(barrier, inc=1, device_id=peer, device_id_type=MESH)
+
+    lane = lax.broadcasted_iota(jnp.int32, (8, 128), 1)
+    rank = jnp.full((8, 128), 64, jnp.int32)
+    for b in range(64):
+        rank = jnp.where(lane == slots[b], b, rank)
+    ranks[...] = rank
+
+    def load(src, dst, n):
+        copy = pltpu.make_async_copy(src, dst, sem_in.at[n])
+        copy.start()
+        return copy
+
+    load_blocks = load(grad, blocks.at[pl.ds(0, 64)], 0)
+    for j in range(3):
+        for k in range(4):
+            load(left_root.at[j, :, pl.ds(k * SHARE, SHARE)], roots.at[j * 16 + k * 4 + y], 1)
+            load(right_root.at[j, :, pl.ds(k * SHARE, SHARE)], rown.at[j * 4 + k], 2)
+    load_table = load(ranks, table, 7)
+    load_cols = load(grad.at[:, :, pl.ds(pl.multiple_of(y * SHARE, SHARE), SHARE)], cols, 3)
+    load_sec = load(second, sec, 4)
+    load_left = load(left, lstat, 5)
+    load_right = load(right, rstat, 6)
+
     blocks[64] = jnp.zeros((ROWS, ORDER), BF16)
-    pl.semaphore_wait(barrier, 30)
+
 
     def to_handler(j, route, piece, zs, xs, other):
         cc = (y + j) % 2
         ff = device(other, x, cc) if route == 0 else device(z, other, cc)
         move(piece, whole.at[j, route, zs, xs, c], sem_gs.at[j], sem_g.at[j], ff)
 
-    def send_grad(j):
+    def pack_grad(j):
         cc = (y + j) % 2
 
         def pack(n, carry):
             zz, xx = n // 4, n % 4
-            piece = blocks[table[device(zz, xx, cc) * 3 + j]]
+            piece = blocks[table[0, device(zz, xx, cc) * 3 + j]]
             packed[0, j, xx, zz] = piece[:, :512]
             packed[1, j, zz, xx] = piece[:, 512:]
             return carry
 
         lax.fori_loop(0, 16, pack, 0)
+
+    def send_lines(j):
         for d in (1, 3, 2):
             xx, zz = (x + d) % 4, (z + d) % 4
             remote(
@@ -103,6 +113,8 @@
             remote(
                 packed.at[1, j, zz], passing.at[1, j, z], sem_g1s.at[j], sem_g1.at[1, j, z], device(zz, x, c), y
             ).start()
+
+    def send_own(j):
         for d in (1, 3, 2, 0):
             xx, zz = (x + d) % 4, (z + d) % 4
             to_handler(j, 0, packed.at[0, j, x, zz], z, x, zz)
@@ -161,16 +173,37 @@
         part = jnp.sum(value * value, axis=0, keepdims=True)
         sham[pl.ds(f * 3 + j, 1), :] = part[:, :128] + part[:, 128:256] + part[:, 256:384] + part[:, 384:]
 
-    def send_part(j):
+    def direct_first(j):
+        wait_units(6, sem_r.at[j])
+        wait_units(32, sem_g.at[j])
+        direct_one(j, rnext, 0, give)
+
+    def direct_one(j, root, n, out):
+        at = slice(n * SHARE, (n + 1) * SHARE)
+        lhs = jnp.concatenate([whole[j, h].reshape(ORDER, 512) for h in (0, 1)], axis=1)
+        rhs = jnp.concatenate([root[j * 4 + k] for k in range(4)], axis=1)
+        half[:, at] = lax.dot_general(lhs, rhs, NT, preferred_element_type=F32).astype(BF16)
+        lhs = jnp.concatenate(
+            [roots[j * 16 + k * 4 : j * 16 + k * 4 + 4].reshape(ORDER, SHARE) for k in range(4)], axis=1
+        )
+        value = jnp.dot(lhs, half[:, at], preferred_element_type=F32)
+        for h in (0, 1):
+            out[j, h] = value[:, h * 128 : (h + 1) * 128].astype(BF16).reshape(4, 4, 2, ROWS, 128)
+        part = jnp.sum(value * value, axis=0, keepdims=True)
+        sham[pl.ds(f * 3 + j, 1), :] += part[:, :128] + part[:, 128:]
+
+    def direct_second(j):
+        direct_one(j, rown, 1, mine)
+
+    def send_give(j):
         for d in (1, 3, 2):
             xx, zz = (x + d) % 4, (z + d) % 4
-            for src, yy in ((give, up), (mine, y)):
-                remote(
-                    src.at[j, 0, :, xx], relayed.at[0, j, 4 - d], sem_s1s.at[j], sem_s1.at[0, j], device(z, xx, c), yy
-                ).start()
-                remote(
-                    src.at[j, 1, zz], relayed.at[1, j, 4 - d], sem_s1s.at[j], sem_s1.at[1, j], device(zz, x, c), yy
-                ).start()
+            remote(
+                give.at[j, 0, :, xx], relayed.at[0, j, 4 - d], sem_s1s.at[j], sem_s1.at[0, j], device(z, xx, c), up
+            ).start()
+            remote(
+                give.at[j, 1, zz], relayed.at[1, j, 4 - d], sem_s1s.at[j], sem_s1.at[1, j], device(zz, x, c), up
+            ).start()
         for d in (1, 3, 2, 0):
             xx, zz = (x + d) % 4, (z + d) % 4
             for cc in (0, 1):
@@ -180,6 +213,19 @@
                 remote(
                     give.at[j, 1, z, xx, cc], got.at[1, j, x, 0, c], sem_hs.at[j], sem_s, device(z, xx, cc), up
                 ).start()
+
+    def send_mine(j):
+        for d in (1, 3, 2):
+            xx, zz = (x + d) % 4, (z + d) % 4
+            remote(
+                mine.at[j, 0, :, xx], relayed.at[0, j, 4 - d], sem_s1s.at[j], sem_s1.at[0, j], device(z, xx, c), y
+            ).start()
+            remote(
+                mine.at[j, 1, zz], relayed.at[1, j, 4 - d], sem_s1s.at[j], sem_s1.at[1, j], device(zz, x, c), y
+            ).start()
+        for d in (1, 3, 2, 0):
+            xx, zz = (x + d) % 4, (z + d) % 4
+            for cc in (0, 1):
                 move(mine.at[j, 0, zz, x, cc], got.at[0, j, z, 0, c], sem_os.at[j], sem_s, device(zz, x, cc))
                 move(mine.at[j, 1, z, xx, cc], got.at[1, j, x, 0, c], sem_os.at[j], sem_s, device(z, xx, cc))
 
@@ -202,40 +248,53 @@
                     device(z, xx, cc),
                 )
 
-    def left_rows(j, r):
-        value = lax.dot_general(rows_at(j, 0, r), whole[j, 0].reshape(ORDER, 512), NT, preferred_element_type=F32)
-        value += lax.dot_general(rows_at(j, 1, r), whole[j, 1].reshape(ORDER, 512), NT, preferred_element_type=F32)
+    def left_part(j, r, h):
+        value = lax.dot_general(
+            rows_at(j, 0, r), whole[j, 0, 2 * h : 2 * h + 2].reshape(512, 512), NT, preferred_element_type=F32
+        )
+        value += lax.dot_general(
+            rows_at(j, 1, r), whole[j, 1, 2 * h : 2 * h + 2].reshape(512, 512), NT, preferred_element_type=F32
+        )
         return value
 
-    def right_rows(j, r):
+    def right_parts(j, r):
         at = pl.ds(pl.multiple_of((r % 2) * SHARE, SHARE), SHARE)
         lhs = whole[j, r // 2, :, :, :, :, at].reshape(ORDER, SHARE).T
         return [jnp.dot(lhs, whole[j, h].reshape(ORDER, 512), preferred_element_type=F32) for h in (0, 1)]
 
-    def next_left(j):
-        stat_out[j, 0] = left_rows(j, up).astype(BF16)
+    def left_up(j):
+        stat_out[j, 0] = left_part(j, up, 0).astype(BF16)
         remote(stat_out.at[j, 0], stat_in.at[j, 0], sem_ps.at[j], sem_p.at[j], f, up).start()
 
+    def left_down(j):
+        stat_out[j, 1] = left_part(j, down, 1).astype(BF16)
+        remote(stat_out.at[j, 1], stat_in.at[j, 1], sem_qs.at[j], sem_q.at[j], f, down).start()
+
     def next_right(j):
-        for h, value in enumerate(right_rows(j, down)):
-            stat_out[j, 1, :, h * 512 : (h + 1) * 512] = value.astype(BF16)
-        remote(stat_out.at[j, 1], stat_in.at[j, 1], sem_qs.at[j], sem_q.at[j], f, down).start()
+        both = pl.ds(2, 2)
+        for h, value in enumerate(right_parts(j, down)):
+            stat_out[j, 2 + h] = value.astype(BF16)
+        remote(stat_out.at[j, both], stat_in.at[j, both], sem_qs.at[j], sem_q.at[j], f, down).start()
 
     def own_left(j):
-        lstat[j] = 0.9 * lstat[j] + 0.1 * left_rows(j, y)
+        for h in (0, 1):
+            at = slice(h * 512, (h + 1) * 512)
+            lstat[j, :, at] = 0.9 * lstat[j, :, at] + 0.1 * left_part(j, y, h)
 
     def own_right(j):
-        for h, value in enumerate(right_rows(j, y)):
+        for h, value in enumerate(right_parts(j, y)):
             at = slice(h * 512, (h + 1) * 512)
             rstat[j, :, at] = 0.9 * rstat[j, :, at] + 0.1 * value
 
-    def receive_left(j):
-        wait_units(8, sem_p.at[j])
-        lstat[j] = 0.9 * lstat[j] + 0.1 * stat_in[j, 0].astype(F32)
-
-    def receive_right(j):
-        wait_units(8, sem_q.at[j])
-        rstat[j] = 0.9 * rstat[j] + 0.1 * stat_in[j, 1].astype(F32)
+    def receive_up(j):
+        wait_units(4, sem_p.at[j])
+        lstat[j, :, :512] = 0.9 * lstat[j, :, :512] + 0.1 * stat_in[j, 0].astype(F32)
+
+    def receive_down(j):
+        wait_units(12, sem_q.at[j])
+        lstat[j, :, 512:] = 0.9 * lstat[j, :, 512:] + 0.1 * stat_in[j, 1].astype(F32)
+        rstat[j, :, :512] = 0.9 * rstat[j, :, :512] + 0.1 * stat_in[j, 2].astype(F32)
+        rstat[j, :, 512:] = 0.9 * rstat[j, :, 512:] + 0.1 * stat_in[j, 3].astype(F32)
 
     stages = [x_line, z_line, y_line]
 
@@ -273,15 +332,19 @@
                 wait_bytes(blocks.at[pl.ds(0, 7), pl.ds(0, 16), pl.ds(0, 512)], sem_os.at[j])
                 wait_units(12, sem_gs.at[j])
                 wait_units(2, sem_ls.at[j])
-                wait_units(8, sem_ps.at[j])
-                wait_units(8, sem_qs.at[j])
+                wait_units(4, sem_ps.at[j])
+                wait_units(12, sem_qs.at[j])
             else:
                 wait_units(16, sem_gs.at[j])
                 wait_units(6, sem_rs.at[j])
                 wait_units(10, sem_ls.at[j])
 
     load_blocks.wait()
-    send_grad(0)
+    load_table.wait()
+    pack_grad(0)
+    pl.semaphore_wait(barrier, 30)
+    send_lines(0)
+    send_own(0)
     wait_units(24, sem_in.at[1])
     wait_units(24, sem_in.at[2])
 
@@ -313,67 +376,79 @@
     lax.fori_loop(0, 64, adam_block, 0)
     load_left.wait()
     load_right.wait()
+    pack_grad(1)
+    pack_grad(2)
     relay_grad(0)
 
     @pl.when((y + c) % 2 == 0)
     def _():
-        send_grad(1)
+        send_lines(1)
+        send_own(1)
         fill(0)
         relay_grad(1)
-        send_grad(2)
+        send_lines(2)
+        send_own(2)
         direct(0)
-        next_left(0)
+        send_give(0)
+        left_up(0)
+        left_down(0)
         next_right(0)
         own_left(0)
         own_right(0)
         fill(2)
         relay_grad(2)
-        send_part(0)
+        send_mine(0)
+        relay_part(0)
         direct(2)
-        send_part(2)
         start_sums()
-        relay_part(0)
+        send_give(2)
+        send_mine(2)
         next_right(2)
-        next_left(2)
+        left_down(2)
         relay_part(1)
         end_stage(0)
         start_stage(1)
         own_left(2)
         own_right(2)
+        left_up(2)
+        relay_part(2)
         end_stage(1)
         start_stage(2)
-        receive_left(1)
-        receive_right(1)
-        relay_part(2)
+        receive_up(1)
+        receive_down(1)
         end_stage(2)
         wait_sent((0, 2))
 
     @pl.when((y + c) % 2 == 1)
     def _():
-        send_grad(1)
+        send_lines(1)
+        send_own(1)
         send_roots(2, False)
         fill(1)
         relay_grad(1)
-        send_grad(2)
+        send_lines(2)
+        send_own(2)
         relay_grad(2)
         direct(1)
-        send_part(1)
-        next_left(1)
+        start_sums()
+        send_give(1)
+        send_mine(1)
+        left_up(1)
+        left_down(1)
         next_right(1)
-        start_sums()
         relay_part(0)
         own_left(1)
         own_right(1)
         relay_part(1)
         end_stage(0)
         start_stage(1)
-        receive_left(0)
-        receive_right(0)
+        receive_up(0)
+        receive_down(0)
+        relay_part(2)
         end_stage(1)
         start_stage(2)
-        relay_part(2)
-        receive_left(2)
-        receive_right(2)
+        receive_down(2)
+        receive_up(2)
         end_stage(2)
         wait_sent((1,))
 
@@ -417,9 +492,6 @@
 def per_device(grad, second, left, right, left_root, right_root, slot_of_block):
     any_space, vmem = pl.BlockSpec(memory_space=pl.ANY), pl.BlockSpec(memory_space=pltpu.VMEM)
     smem = pl.BlockSpec(memory_space=pltpu.SMEM)
-    slots = jnp.arange(96, dtype=jnp.int32)
-    named = slot_of_block[None, :] == slots[:, None]
-    table = jnp.min(jnp.where(named, jnp.arange(64, dtype=jnp.int32)[None, :], 64), axis=1)
     dma = pltpu.SemaphoreType.DMA
     lstat, rstat, sec, got, sums = pl.pallas_call(
         exchange_kernel,
@@ -434,6 +506,8 @@
         in_specs=[smem] + [any_space] * 6,
         out_specs=(vmem,) * 5,
         scratch_shapes=[
+            pltpu.SMEM((8, 128), jnp.int32),
+            pltpu.VMEM((8, 128), jnp.int32),
             pltpu.VMEM((65, 32, 1024), BF16),
             pltpu.VMEM((64, 32, 256), BF16),
             pltpu.VMEM((2, 3, 4, 4, 32, 512), BF16),
@@ -446,13 +520,13 @@
             pltpu.VMEM((3, 2, 4, 4, 2, 32, 128), BF16),
             pltpu.VMEM((3, 2, 4, 4, 2, 32, 128), BF16),
             pltpu.VMEM((2, 3, 4, 4, 2, 32, 128), BF16),
-            pltpu.VMEM((3, 2, 256, 1024), BF16),
-            pltpu.VMEM((3, 2, 256, 1024), BF16),
+            pltpu.VMEM((3, 4, 256, 512), BF16),
+            pltpu.VMEM((3, 4, 256, 512), BF16),
             pltpu.VMEM((128, 128), F32),
             pltpu.VMEM((128, 128), F32),
             pltpu.VMEM((4, 8, 128), F32),
             pltpu.VMEM((3, 7, 8, 128), F32),
-            dma((7,)),
+            dma((8,)),
             dma((2, 3, 4)), dma((3,)),
             dma((3,)), dma((3,)),
             dma((3,)), dma((3,)),
@@ -467,7 +541,7 @@
         compiler_params=pltpu.CompilerParams(
             collective_id=0, has_side_effects=True, vmem_limit_bytes=EXCHANGE_VMEM
         ),
-    )(table, grad, second, left, right, left_root, right_root)
+    )(slot_of_block, grad, second, left, right, left_root, right_root)
     return pl.pallas_call(
         finish_kernel,
         name="finish",

time: 75.4 us -> 73.2 us (0.971)
  other arithmetic: 1.26 us -> 0 us
  Pallas kernels: 73.2 us -> 72.3 us
    reduce_min x1 -> x0, other arithmetic: 1.26 us -> none  [per_device(): jnp.min(jnp.where(named, jnp.arange(64, dtype=jnp.int32)[None, :], 64), a...]
    pallas_call x1, Pallas kernels: 68.6 us -> 67.7 us  [per_device(): pl.pallas_call(exchange_kernel, name='exchange', out_shape=(pltpu.VMEM((3...]
where the time goes in v4:
time: 73.2 us; the launch traced here: 73.1 us
  Pallas kernels  72.3 us (99%)
  between operations  0.84 us (1%)
    pallas_call x1, Pallas kernels, per_device(): pl.pallas_call(exchange_kernel, name='exchange', out_shape=(pltpu.VMEM((3...  67.7 us
    pallas_call x1, Pallas kernels, per_device(): pl.pallas_call(finish_kernel, name='finish', out_shape=(jax.ShapeDtypeStr...  4.58 us

profile of v4, /device:TPU:1, one launch (start us, length us, event | category | flops | bytes accessed | tf_op | source)
XLA Modules:
  0.0 73.1 jit_solution(15147198389305817339)
XLA Ops:
  0.6 0.0 copy-start
  0.6 67.7 %exchange.1 = (f32[3,256,1024]{2,1,0:T(8,128)S(1)}, f32[3,256,1024]{2,1,0:T(8,128)S(1)}, f32[64,32,256]{2,1,0:T(8,128)S(1)}, bf16[2,3,4,4,2,32,128]{6,5,4,3,2,1,0:T(8,128)(2,1)S(1)}, f32[8,128]{1,0:T(8,128)S(1)}) custom-call(s32[64]{0:T(128)} %slots.3, bf16[64,32,1024]{2,1,0:T(8,128)(2,1)} %grad.1, f32[64,32,256]{2,1,0:T(8,128)} %second.1, ...), custom_call_target="tpu_custom_call" | custom-call | tf_op jit(solution)/shard_map/exchange/pallas_call | solution.py:496
  68.4 0.0 copy-done
  68.4 4.6 %finish.1 = (f32[3,256,1024]{2,1,0:T(8,128)}, f32[3,256,1024]{2,1,0:T(8,128)}, f32[64,32,256]{2,1,0:T(8,128)}, f32[64,32,256]{2,1,0:T(8,128)}) custom-call(s32[64]{0:T(128)S(1)} %copy-done, f32[3,256,1024]{2,1,0:T(8,128)S(1)} %get-tuple-element.9.lstat, f32[3,256,1024]{2,1,0:T(8,128)S(1)} %get-tuple-element.10.rstat, ...), custom_call_target="tpu_custom_call" | custom-call | tf_op jit(solution)/shard_map/finish/pallas_call | solution.py:545
Async XLA Ops:
  0.6 67.7 %copy-start = (s32[64]{0:T(128)S(1)}, s32[64]{0:T(128)}, u32[]{:S(2)}) copy-start(s32[64]{0:T(128)} %slots.3) | copy-start | bytes 772

commit v5 on v4

--- a/solution.py
+++ b/solution.py
@@ -19,7 +19,7 @@
     table, ranks, blocks, cols, packed, passing, whole, roots, rown, rnext, half,
     mine, give, relayed, stat_out, stat_in, adam, sham, tile, tiles_in,
     sem_in, sem_g1, sem_g1s, sem_g, sem_gs, sem_l, sem_ls, sem_r, sem_rs,
-    sem_os, sem_hs, sem_s1, sem_s1s, sem_s, sem_ss, sem_p, sem_ps, sem_q, sem_qs, sem_t, sem_ts,
+    sem_s1, sem_s1s, sem_s, sem_ss, sem_p, sem_ps, sem_q, sem_qs, sem_t, sem_ts,
 ):
     f, y = lax.axis_index("fsdp"), lax.axis_index("grp")
     c, x, z = f % 2, (f // 2) % 4, f // 8
@@ -55,9 +55,8 @@
     z_other = [(device((z + d) % 4, x, 1 - c), y) for d in (1, 2, 3)]
     y_line = [(f, (y + d) % 4) for d in (1, 2, 3)]
     senders = x_line + z_line + z_other + y_line
-    for cc, yy in ((0, (y + 3) % 4), (1, (y + 1) % 4)):
-        senders += [(device(z, (x + d) % 4, cc), yy) for d in (0, 1, 2, 3)]
-        senders += [(device((z + d) % 4, x, cc), yy) for d in (1, 2, 3)]
+    senders += [(device(z, (x + d) % 4, c), down) for d in (1, 2, 3)]
+    senders += [(device((z + d) % 4, x, c), down) for d in (1, 2, 3)]
     barrier = pltpu.get_barrier_semaphore()
     for peer in senders:
         pl.semaphore_signal(barrier, inc=1, device_id=peer, device_id_type=MESH)
@@ -120,8 +119,8 @@
             to_handler(j, 0, packed.at[0, j, x, zz], z, x, zz)
             to_handler(j, 1, packed.at[1, j, z, xx], z, x, xx)
 
-    def relay_grad(j):
-        for e in (1, 3, 2):
+    def relay_grad(j, distances=(1, 3, 2)):
+        for e in distances:
             xs, zs = (x + e) % 4, (z + e) % 4
             wait_units(2, sem_g1.at[0, j, xs])
             for d in (1, 3, 2, 0):
@@ -167,52 +166,22 @@
         )
         value = jnp.dot(lhs, half[...], preferred_element_type=F32)
         for n, out in enumerate((give, mine)):
-            for h in (0, 1):
-                at = n * SHARE + h * 128
-                out[j, h] = value[:, at : at + 128].astype(BF16).reshape(4, 4, 2, ROWS, 128)
+            piece = value[:, n * SHARE : (n + 1) * SHARE].astype(BF16).reshape(4, 4, 2, ROWS, SHARE)
+            out[j, 0] = piece[:, :, 0]
+            out[j, 1] = piece[:, :, 1]
         part = jnp.sum(value * value, axis=0, keepdims=True)
         sham[pl.ds(f * 3 + j, 1), :] = part[:, :128] + part[:, 128:256] + part[:, 256:384] + part[:, 384:]
 
-    def direct_first(j):
-        wait_units(6, sem_r.at[j])
-        wait_units(32, sem_g.at[j])
-        direct_one(j, rnext, 0, give)
-
-    def direct_one(j, root, n, out):
-        at = slice(n * SHARE, (n + 1) * SHARE)
-        lhs = jnp.concatenate([whole[j, h].reshape(ORDER, 512) for h in (0, 1)], axis=1)
-        rhs = jnp.concatenate([root[j * 4 + k] for k in range(4)], axis=1)
-        half[:, at] = lax.dot_general(lhs, rhs, NT, preferred_element_type=F32).astype(BF16)
-        lhs = jnp.concatenate(
-            [roots[j * 16 + k * 4 : j * 16 + k * 4 + 4].reshape(ORDER, SHARE) for k in range(4)], axis=1
-        )
-        value = jnp.dot(lhs, half[:, at], preferred_element_type=F32)
-        for h in (0, 1):
-            out[j, h] = value[:, h * 128 : (h + 1) * 128].astype(BF16).reshape(4, 4, 2, ROWS, 128)
-        part = jnp.sum(value * value, axis=0, keepdims=True)
-        sham[pl.ds(f * 3 + j, 1), :] += part[:, :128] + part[:, 128:]
-
-    def direct_second(j):
-        direct_one(j, rown, 1, mine)
-
     def send_give(j):
-        for d in (1, 3, 2):
+        for d in (1, 3, 2, 0):
             xx, zz = (x + d) % 4, (z + d) % 4
+            e = (4 - d) % 4
             remote(
-                give.at[j, 0, :, xx], relayed.at[0, j, 4 - d], sem_s1s.at[j], sem_s1.at[0, j], device(z, xx, c), up
+                give.at[j, 0, :, xx], relayed.at[0, j, e], sem_s1s.at[j], sem_s1.at[0, j], device(z, xx, c), up
             ).start()
             remote(
-                give.at[j, 1, zz], relayed.at[1, j, 4 - d], sem_s1s.at[j], sem_s1.at[1, j], device(zz, x, c), up
+                give.at[j, 1, zz], relayed.at[1, j, e], sem_s1s.at[j], sem_s1.at[1, j], device(zz, x, c), up
             ).start()
-        for d in (1, 3, 2, 0):
-            xx, zz = (x + d) % 4, (z + d) % 4
-            for cc in (0, 1):
-                remote(
-                    give.at[j, 0, zz, x, cc], got.at[0, j, z, 0, c], sem_hs.at[j], sem_s, device(zz, x, cc), up
-                ).start()
-                remote(
-                    give.at[j, 1, z, xx, cc], got.at[1, j, x, 0, c], sem_hs.at[j], sem_s, device(z, xx, cc), up
-                ).start()
 
     def send_mine(j):
         for d in (1, 3, 2):
@@ -223,30 +192,18 @@
             remote(
                 mine.at[j, 1, zz], relayed.at[1, j, 4 - d], sem_s1s.at[j], sem_s1.at[1, j], device(zz, x, c), y
             ).start()
-        for d in (1, 3, 2, 0):
-            xx, zz = (x + d) % 4, (z + d) % 4
-            for cc in (0, 1):
-                move(mine.at[j, 0, zz, x, cc], got.at[0, j, z, 0, c], sem_os.at[j], sem_s, device(zz, x, cc))
-                move(mine.at[j, 1, z, xx, cc], got.at[1, j, x, 0, c], sem_os.at[j], sem_s, device(z, xx, cc))
+        pltpu.make_async_copy(mine.at[j, 0, :, x], relayed.at[0, j, 0], sem_s1.at[0, j]).start()
+        pltpu.make_async_copy(mine.at[j, 1, z], relayed.at[1, j, 0], sem_s1.at[1, j]).start()
 
     def relay_part(j):
-        others = pl.ds(1, 3)
-        wait_units(3, sem_s1.at[0, j])
+        wait_units(4, sem_s1.at[0, j])
         for d in (1, 3, 2, 0):
             zz = (z + d) % 4
-            for cc in (0, 1):
-                move(
-                    relayed.at[0, j, others, zz, cc], got.at[0, j, z, others, c], sem_ss.at[j], sem_s,
-                    device(zz, x, cc),
-                )
-        wait_units(3, sem_s1.at[1, j])
+            move(relayed.at[0, j, :, zz], got.at[j, z, :, c], sem_ss.at[j], sem_s, device(zz, x, 0))
+        wait_units(4, sem_s1.at[1, j])
         for d in (1, 3, 2, 0):
             xx = (x + d) % 4
-            for cc in (0, 1):
-                move(
-                    relayed.at[1, j, others, xx, cc], got.at[1, j, x, others, c], sem_ss.at[j], sem_s,
-                    device(z, xx, cc),
-                )
+            move(relayed.at[1, j, :, xx], got.at[j, x, :, c], sem_ss.at[j], sem_s, device(z, xx, 1))
 
     def left_part(j, r, h):
         value = lax.dot_general(
@@ -325,11 +282,9 @@
     def wait_sent(handled):
         for j in range(3):
             wait_units(12, sem_g1s.at[j])
-            wait_bytes(blocks.at[pl.ds(0, 21), pl.ds(0, 16), pl.ds(0, 512)], sem_ss.at[j])
+            wait_units(7, sem_ss.at[j])
             if j in handled:
-                wait_units(12, sem_s1s.at[j])
-                wait_units(2, sem_hs.at[j])
-                wait_bytes(blocks.at[pl.ds(0, 7), pl.ds(0, 16), pl.ds(0, 512)], sem_os.at[j])
+                wait_units(14, sem_s1s.at[j])
                 wait_units(12, sem_gs.at[j])
                 wait_units(2, sem_ls.at[j])
                 wait_units(4, sem_ps.at[j])
@@ -342,7 +297,7 @@
     load_blocks.wait()
     load_table.wait()
     pack_grad(0)
-    pl.semaphore_wait(barrier, 30)
+    pl.semaphore_wait(barrier, 22)
     send_lines(0)
     send_own(0)
     wait_units(24, sem_in.at[1])
@@ -373,12 +328,12 @@
         adam[pl.ds(b, 1), :] = part[:, :128] + part[:, 128:]
         return carry
 
-    lax.fori_loop(0, 64, adam_block, 0)
     load_left.wait()
     load_right.wait()
     pack_grad(1)
     pack_grad(2)
     relay_grad(0)
+    lax.fori_loop(0, 64, adam_block, 0)
 
     @pl.when((y + c) % 2 == 0)
     def _():
@@ -398,11 +353,11 @@
         fill(2)
         relay_grad(2)
         send_mine(0)
-        relay_part(0)
         direct(2)
         start_sums()
         send_give(2)
         send_mine(2)
+        relay_part(0)
         next_right(2)
         left_down(2)
         relay_part(1)
@@ -464,27 +419,29 @@
         stores.append(copy)
 
     f = lax.axis_index("fsdp")
-    x, z = (f // 2) % 4, f // 8
+    core, x, z = f % 2, (f // 2) % 4, f // 8
     for n in (0, 1):
         rows[n] = jnp.broadcast_to(sums[n : n + 1, :], (128, 128)).T
-
-    def one(b, carry):
+    for b in range(64):
+        rows[2, b : b + 1, :] = rows[1, pl.ds(slots[b], 1), :]
+    adam_sq = rows[0, :64] * (1.0 / 1048576.0)
+    sham_sq = rows[2, :64] * (1.0 / 1048576.0)
+    rows[3, :64] = jnp.sqrt(adam_sq / (sham_sq + 1e-06))
+
+    for b in range(64):
         slot = slots[b]
         j, owner = slot % 3, slot // 3
         c, xs, zs = owner % 2, (owner // 2) % 4, owner // 8
-        adam_sq = rows[0, pl.ds(b, 1), :] * (1.0 / 1048576.0)
-        sham_sq = rows[1, pl.ds(slot, 1), :] * (1.0 / 1048576.0)
-        factor = jnp.sqrt(adam_sq / (sham_sq + 1e-06))
-        wide[b, :, :128] = got[0, j, zs, (xs + 4 - x) % 4, c].astype(F32) * factor
-        wide[b, :, 128:] = got[1, j, xs, (zs + 4 - z) % 4, c].astype(F32) * factor
-        return carry
-
-    for n in range(4):
-        part = pl.ds(n * 16, 16)
-        lax.fori_loop(n * 16, n * 16 + 16, one, 0)
-        copy = pltpu.make_async_copy(wide.at[part], out.at[part], sem.at[3 + n])
-        copy.start()
-        stores.append(copy)
+        first = zs + core * (xs - zs)
+        rest = (xs - x + core * (zs - z - xs + x) + 8) % 4
+        factor = rows[3, b : b + 1, :]
+        wide[b, :, :128] = got[j, first, rest, c, :, :128].astype(F32) * factor
+        wide[b, :, 128:] = got[j, first, rest, c, :, 128:].astype(F32) * factor
+        if b % 16 == 15:
+            part = pl.ds(b - 15, 16)
+            copy = pltpu.make_async_copy(wide.at[part], out.at[part], sem.at[3 + b // 16])
+            copy.start()
+            stores.append(copy)
     for copy in stores:
         copy.wait()
 
@@ -500,7 +457,7 @@
             pltpu.VMEM((3, 256, 1024), F32),
             pltpu.VMEM((3, 256, 1024), F32),
             pltpu.VMEM((64, 32, 256), F32),
-            pltpu.VMEM((2, 3, 4, 4, 2, 32, 128), BF16),
+            pltpu.VMEM((3, 4, 4, 2, 32, 256), BF16),
             pltpu.VMEM((8, 128), F32),
         ),
         in_specs=[smem] + [any_space] * 6,
@@ -517,9 +474,9 @@
             pltpu.VMEM((12, 256, 256), BF16),
             pltpu.VMEM((12, 256, 256), BF16),
             pltpu.VMEM((1024, 512), BF16),
-            pltpu.VMEM((3, 2, 4, 4, 2, 32, 128), BF16),
-            pltpu.VMEM((3, 2, 4, 4, 2, 32, 128), BF16),
-            pltpu.VMEM((2, 3, 4, 4, 2, 32, 128), BF16),
+            pltpu.VMEM((3, 2, 4, 4, 32, 256), BF16),
+            pltpu.VMEM((3, 2, 4, 4, 32, 256), BF16),
+            pltpu.VMEM((2, 3, 4, 4, 32, 256), BF16),
             pltpu.VMEM((3, 4, 256, 512), BF16),
             pltpu.VMEM((3, 4, 256, 512), BF16),
             pltpu.VMEM((128, 128), F32),
@@ -528,7 +485,6 @@
             pltpu.VMEM((3, 7, 8, 128), F32),
             dma((8,)),
             dma((2, 3, 4)), dma((3,)),
-            dma((3,)), dma((3,)),
             dma((3,)), dma((3,)),
             dma((3,)), dma((3,)),
             dma((3,)), dma((3,)),
@@ -553,7 +509,7 @@
         ),
         in_specs=[smem] + [vmem] * 5,
         out_specs=(any_space,) * 4,
-        scratch_shapes=[pltpu.VMEM((64, 32, 256), F32), pltpu.VMEM((2, 128, 128), F32), dma((7,))],
+        scratch_shapes=[pltpu.VMEM((64, 32, 256), F32), pltpu.VMEM((4, 128, 128), F32), dma((7,))],
         compiler_params=pltpu.CompilerParams(vmem_limit_bytes=FINISH_VMEM),
     )(slot_of_block, lstat, rstat, sec, got, sums)
 

time: 73.2 us -> 72.2 us (0.986)
  Pallas kernels: 72.3 us -> 71.2 us
    pallas_call x1, Pallas kernels: 67.7 us -> 66.7 us  [per_device(): pl.pallas_call(exchange_kernel, name='exchange', out_shape=(pltpu.VMEM((3...]
where the time goes in v5:
time: 72.2 us; the launch traced here: 72.1 us
  Pallas kernels  71.2 us (99%)
  between operations  0.84 us (1%)
    pallas_call x1, Pallas kernels, per_device(): pl.pallas_call(exchange_kernel, name='exchange', out_shape=(pltpu.VMEM((3...  66.7 us
    pallas_call x1, Pallas kernels, per_device(): pl.pallas_call(finish_kernel, name='finish', out_shape=(jax.ShapeDtypeStr...  4.57 us

profile of v5, /device:TPU:1, one launch (start us, length us, event | category | flops | bytes accessed | tf_op | source)
XLA Modules:
  0.0 72.1 jit_solution(207717609253583866)
XLA Ops:
  0.6 0.0 copy-start
  0.6 66.7 %exchange.1 = (f32[3,256,1024]{2,1,0:T(8,128)S(1)}, f32[3,256,1024]{2,1,0:T(8,128)S(1)}, f32[64,32,256]{2,1,0:T(8,128)S(1)}, bf16[3,4,4,2,32,256]{5,4,3,2,1,0:T(8,128)(2,1)S(1)}, f32[8,128]{1,0:T(8,128)S(1)}) custom-call(s32[64]{0:T(128)} %slots.3, bf16[64,32,1024]{2,1,0:T(8,128)(2,1)} %grad.1, f32[64,32,256]{2,1,0:T(8,128)} %second.1, ...), custom_call_target="tpu_custom_call" | custom-call | tf_op jit(solution)/shard_map/exchange/pallas_call | solution.py:453
  67.3 0.0 copy-done
  67.3 4.6 %finish.1 = (f32[3,256,1024]{2,1,0:T(8,128)}, f32[3,256,1024]{2,1,0:T(8,128)}, f32[64,32,256]{2,1,0:T(8,128)}, f32[64,32,256]{2,1,0:T(8,128)}) custom-call(s32[64]{0:T(128)S(1)} %copy-done, f32[3,256,1024]{2,1,0:T(8,128)S(1)} %get-tuple-element.9.lstat, f32[3,256,1024]{2,1,0:T(8,128)S(1)} %get-tuple-element.10.rstat, ...), custom_call_target="tpu_custom_call" | custom-call | tf_op jit(solution)/shard_map/finish/pallas_call | solution.py:501
Async XLA Ops:
  0.6 66.7 %copy-start = (s32[64]{0:T(128)S(1)}, s32[64]{0:T(128)}, u32[]{:S(2)}) copy-start(s32[64]{0:T(128)} %slots.3) | copy-start | bytes 772

commit v6 on v5

--- a/solution.py
+++ b/solution.py
@@ -340,11 +340,11 @@
         send_lines(1)
         send_own(1)
         fill(0)
+        direct(0)
+        send_give(0)
         relay_grad(1)
         send_lines(2)
         send_own(2)
-        direct(0)
-        send_give(0)
         left_up(0)
         left_down(0)
         next_right(0)

time: 72.2 us -> 71.9 us (level)
  no operation moved by 1% of the time
where the time goes in v6:
time: 71.9 us; the launch traced here: 71.8 us
  Pallas kernels  71 us (99%)
  between operations  0.84 us (1%)
    pallas_call x1, Pallas kernels, per_device(): pl.pallas_call(exchange_kernel, name='exchange', out_shape=(pltpu.VMEM((3...  66.4 us
    pallas_call x1, Pallas kernels, per_device(): pl.pallas_call(finish_kernel, name='finish', out_shape=(jax.ShapeDtypeStr...  4.57 us

profile of v6, /device:TPU:1, one launch (start us, length us, event | category | flops | bytes accessed | tf_op | source)
XLA Modules:
  0.0 71.8 jit_solution(15795254858991415907)
XLA Ops:
  0.6 0.0 copy-start
  0.6 66.4 %exchange.1 = (f32[3,256,1024]{2,1,0:T(8,128)S(1)}, f32[3,256,1024]{2,1,0:T(8,128)S(1)}, f32[64,32,256]{2,1,0:T(8,128)S(1)}, bf16[3,4,4,2,32,256]{5,4,3,2,1,0:T(8,128)(2,1)S(1)}, f32[8,128]{1,0:T(8,128)S(1)}) custom-call(s32[64]{0:T(128)} %slots.3, bf16[64,32,1024]{2,1,0:T(8,128)(2,1)} %grad.1, f32[64,32,256]{2,1,0:T(8,128)} %second.1, ...), custom_call_target="tpu_custom_call" | custom-call | tf_op jit(solution)/shard_map/exchange/pallas_call | solution.py:453
  67.0 0.0 copy-done
  67.1 4.6 %finish.1 = (f32[3,256,1024]{2,1,0:T(8,128)}, f32[3,256,1024]{2,1,0:T(8,128)}, f32[64,32,256]{2,1,0:T(8,128)}, f32[64,32,256]{2,1,0:T(8,128)}) custom-call(s32[64]{0:T(128)S(1)} %copy-done, f32[3,256,1024]{2,1,0:T(8,128)S(1)} %get-tuple-element.9.lstat, f32[3,256,1024]{2,1,0:T(8,128)S(1)} %get-tuple-element.10.rstat, ...), custom_call_target="tpu_custom_call" | custom-call | tf_op jit(solution)/shard_map/finish/pallas_call | solution.py:501
Async XLA Ops:
  0.6 66.4 %copy-start = (s32[64]{0:T(128)S(1)}, s32[64]{0:T(128)}, u32[]{:S(2)}) copy-start(s32[64]{0:T(128)} %slots.3) | copy-start | bytes 772
